TPU v7x, 32 devices: a whole 2x2x4 slice. The times are simulated.
32 devices in a mesh: dp: 4 (over y, core), shard: 8 (over z, x).
Axes of the slice: x: 2, y: 2, z: 4, core: 2. Of those that a mesh axis runs over, the one named last changes fastest.
Arguments:
- tokens: bfloat16 [16384, 768], P(('dp', 'shard')), may hold values from -36 to 36
- picture_ids: int32 [16384], P(('dp', 'shard')), may hold values from 0 to 4, as said below
- cotangent: bfloat16 [16384, 768], P(('dp', 'shard')), may hold values from -38 to 38
- w_qkv: float32 [768, 2304], P('shard'), may hold values from -0.21875 to 0.21875
- w_out: float32 [768, 768], P('shard'), may hold values from -0.875 to 0.875
- w_fc1: float32 [768, 3072], P('shard'), may hold values from -0.21875 to 0.21875
- w_fc2: float32 [3072, 768], P('shard'), may hold values from -0.109375 to 0.109375
- vectors: float32 [8, 768], P(None, 'shard'), may hold values from -2 to 2
- fc1_bias: float32 [3072], P('shard'), may hold values from -3 to 3
- moments_qkv: float32 [2, 768, 2304], P(None, 'shard'), may hold values from -0.002 to 0.002, as said below
- moments_out: float32 [2, 768, 768], P(None, 'shard'), may hold values from -0.002 to 0.002, as said below
- moments_fc1: float32 [2, 768, 3072], P(None, 'shard'), may hold values from -0.002 to 0.002, as said below
- moments_fc2: float32 [2, 3072, 768], P(None, 'shard'), may hold values from -0.002 to 0.002, as said below
- moments_vectors: float32 [2, 8, 768], P(None, None, 'shard'), may hold values from -0.002 to 0.002, as said below
- moments_fc1_bias: float32 [2, 3072], P(None, 'shard'), may hold values from -0.002 to 0.002, as said below
Outputs:
- layer_out: bfloat16 [16384, 768], P(('dp', 'shard'))
- tokens_grad: bfloat16 [16384, 768], P(('dp', 'shard'))
- grad_qkv: float32 [768, 2304], P('shard')
- grad_out: float32 [768, 768], P('shard')
- grad_fc1: float32 [768, 3072], P('shard')
- grad_fc2: float32 [3072, 768], P('shard')
- grad_vectors: float32 [8, 768], P(None, 'shard')
- grad_fc1_bias: float32 [3072], P('shard')
- new_qkv: float32 [768, 2304], P('shard')
- new_out: float32 [768, 768], P('shard')
- new_fc1: float32 [768, 3072], P('shard')
- new_fc2: float32 [3072, 768], P('shard')
- vectors_step: float32 [8, 768], P(None, 'shard')
- new_fc1_bias: float32 [3072], P('shard')
- stream_rms: float32 [5], replicated
Inputs may be any that keep to these rules, and one draw needn't show every extreme that they name: `picture_ids`: within each row of 512 tokens the pictures are numbered 1, 2, ... from the row's start, one to four a row, each of 100 or more tokens; 0 marks padding, fewer than 100 tokens at a row's end; the first row is one picture of all 512 tokens. `moments_qkv`: the second moments are positive. `moments_out`: the second moments are positive. `moments_fc1`: the second moments are positive. `moments_fc2`: the second moments are positive. `moments_vectors`: the second moments are positive. `moments_fc1_bias`: the second moments are positive.
All inputs are finite; a program needn't handle non-finite values.
Results may differ from a plain program's by a relative error of at most 0.012.
The roundings to bfloat16 on the way count: a program that leaves them out, or rounds other values in their place, can miss the bound.
Values may be sent and summed in bfloat16 or wider, within the bound.
No kernel may reach another device: no remote copies, remote signals or barrier semaphores. Data moves between devices by JAX's collectives and lax.ppermute only.
A program may use at most 256 MiB of HBM per device.

v0:
```python
from functools import partial

import jax
import jax.numpy as jnp
from jax import lax
from jax.sharding import PartitionSpec as P

HEADS = 12
HEAD_DIM = 64
ROW = 512
STEP = 2


NORM_EPS = 1e-06
ADAM_BETA = 0.5
LEARN_RATE = 0.03
WEIGHT_DECAY = 0.1
ADAM_EPS = 1e-08
CLIP_NORM = 1.0
MASKED = -1e30


def layer_norm(entries, scale_row, shift_row):
    center = entries - jnp.mean(entries, axis=-1, keepdims=True)
    spread = jnp.mean(center * center, axis=-1, keepdims=True)
    return center * lax.rsqrt(spread + NORM_EPS) * scale_row + shift_row


def gelu_tanh(entries):
    return jax.nn.gelu(entries, approximate=True)


def block_scores(query_block, key_rows, picture, start_row, block_size, score_scale):
    scores = (
        jnp.einsum("qhd,khd->hqk", query_block, key_rows, preferred_element_type=jnp.float32)
        * score_scale
    )
    same_picture = picture[start_row : start_row + block_size, None] == picture[None, :]
    return jnp.where(same_picture[None], scores, MASKED)


def attend_forward(blocks_in, block_size, score_scale):
    queries, key_rows, values_in, picture = blocks_in
    scores = block_scores(queries, key_rows, picture, 0, block_size, score_scale)
    row_max = jnp.max(scores, axis=-1, keepdims=True)
    weights = jnp.exp(scores - row_max)
    row_total = jnp.sum(weights, axis=-1, keepdims=True)
    weights_low = (weights / row_total).astype(jnp.bfloat16)
    mixtures = [
        jnp.einsum("hqk,khd->qhd", weights_low, values_in, preferred_element_type=jnp.float32)
    ]
    log_totals = [(row_max + jnp.log(row_total))[:, :, 0]]
    return (jnp.concatenate(mixtures, 0), jnp.concatenate(log_totals, 1))


def attend_backward(blocks_in, block_size, score_scale):
    queries, key_rows, values_in, grad_mix, picture, log_total = blocks_in
    grad_keys = jnp.zeros(key_rows.shape, jnp.float32)
    grad_values = jnp.zeros(values_in.shape, jnp.float32)
    scores = block_scores(queries, key_rows, picture, 0, block_size, score_scale)
    weights = jnp.exp(scores - log_total[:, 0:block_size, None])
    grad_weights = jnp.einsum(
        "qhd,khd->hqk", grad_mix, values_in, preferred_element_type=jnp.float32
    )
    row_inner = jnp.sum(weights * grad_weights, axis=-1, keepdims=True)
    grad_scores = (weights * (grad_weights - row_inner)).astype(jnp.bfloat16)
    grad_queries = [
        jnp.einsum("hqk,khd->qhd", grad_scores, key_rows, preferred_element_type=jnp.float32)
        * score_scale
    ]
    grad_keys = (
        grad_keys
        + jnp.einsum("hqk,qhd->khd", grad_scores, queries, preferred_element_type=jnp.float32)
        * score_scale
    )
    grad_values = grad_values + jnp.einsum(
        "hqk,qhd->khd", weights.astype(jnp.bfloat16), grad_mix, preferred_element_type=jnp.float32
    )
    return (jnp.concatenate(grad_queries, 0), grad_keys, grad_values)


def owner_major(gradient, split_dim, shard_count, data_count):
    length = gradient.shape[split_dim]
    split_shape = (
        gradient.shape[:split_dim]
        + (shard_count, data_count, length // (shard_count * data_count))
        + gradient.shape[split_dim + 1 :]
    )
    moved = jnp.swapaxes(gradient.reshape(split_shape), split_dim, split_dim + 1)
    return moved.reshape(gradient.shape)


def body(
    tokens,
    picture_ids,
    cotangent,
    w_qkv,
    w_out,
    w_fc1,
    w_fc2,
    vectors,
    fc1_bias,
    moments_qkv,
    moments_out,
    moments_fc1,
    moments_fc2,
    moments_vectors,
    moments_fc1_bias,
):
    model_width = tokens.shape[1]
    masters = (w_qkv, w_out, w_fc1, w_fc2, vectors, fc1_bias)
    moments = (
        moments_qkv,
        moments_out,
        moments_fc1,
        moments_fc2,
        moments_vectors,
        moments_fc1_bias,
    )
    qkv_low, out_low, fc1_low, fc2_low, vector_low, fc1_bias_low = (
        lax.all_gather(w_qkv.astype(jnp.bfloat16), "shard", axis=0, tiled=True),
        lax.all_gather(w_out.astype(jnp.bfloat16), "shard", axis=0, tiled=True),
        lax.all_gather(w_fc1.astype(jnp.bfloat16), "shard", axis=0, tiled=True),
        lax.all_gather(w_fc2.astype(jnp.bfloat16), "shard", axis=0, tiled=True),
        lax.all_gather(vectors.astype(jnp.bfloat16), "shard", axis=1, tiled=True),
        lax.all_gather(fc1_bias.astype(jnp.bfloat16), "shard", axis=0, tiled=True),
    )
    vector_rows = vector_low.astype(jnp.float32)
    fc1_shift = fc1_bias_low.astype(jnp.float32)
    stream = tokens.astype(jnp.float32)
    normed_one, norm_one_back = jax.vjp(layer_norm, stream, vector_rows[0], vector_rows[1])
    act_one = normed_one.astype(jnp.bfloat16)
    projected = jnp.dot(act_one, qkv_low, preferred_element_type=jnp.float32)
    queries = (projected[:, :model_width] + vector_rows[2]).astype(jnp.bfloat16)
    key_rows = projected[:, model_width : 2 * model_width].astype(jnp.bfloat16)
    values = (projected[:, 2 * model_width :] + vector_rows[3]).astype(jnp.bfloat16)
    row_count = tokens.shape[0] // ROW
    head_shape = (row_count, ROW, HEADS, HEAD_DIM)
    block_size = min(512, ROW)
    score_scale = HEAD_DIM ** (-0.5)
    row_pictures = picture_ids.reshape(row_count, ROW)
    query_heads = queries.reshape(head_shape)
    key_heads = key_rows.reshape(head_shape)
    value_heads = values.reshape(head_shape)
    mixture, log_total = lax.map(
        partial(attend_forward, block_size=block_size, score_scale=score_scale),
        (query_heads, key_heads, value_heads, row_pictures),
    )
    mixture_low = mixture.reshape(-1, model_width).astype(jnp.bfloat16)
    attention = jnp.dot(mixture_low, out_low, preferred_element_type=jnp.float32) + vector_rows[4]
    middle = stream + attention
    normed_two, norm_two_back = jax.vjp(layer_norm, middle, vector_rows[5], vector_rows[6])
    act_two = normed_two.astype(jnp.bfloat16)
    preact = jnp.dot(act_two, fc1_low, preferred_element_type=jnp.float32) + fc1_shift
    hidden, gelu_back = jax.vjp(gelu_tanh, preact)
    hidden_low = hidden.astype(jnp.bfloat16)
    feedforward = jnp.dot(hidden_low, fc2_low, preferred_element_type=jnp.float32) + vector_rows[7]
    result = middle + feedforward
    layer_out = result.astype(jnp.bfloat16)
    valid_rows = (picture_ids != 0).astype(jnp.float32)[:, None]
    stream_local = jnp.stack(
        [
            jnp.sum(valid_rows * entry * entry)
            for entry in (stream, attention, middle, feedforward, result)
        ]
        + [jnp.sum(valid_rows)]
    )
    grad_result = cotangent.astype(jnp.float32)
    grad_fc2_shift = jnp.sum(grad_result, axis=0)
    grad_fc2 = jnp.einsum("tf,td->fd", hidden_low, cotangent, preferred_element_type=jnp.float32)
    grad_hidden = jnp.einsum("td,fd->tf", cotangent, fc2_low, preferred_element_type=jnp.float32)
    grad_preact = gelu_back(grad_hidden)[0]
    grad_fc1_shift = jnp.sum(grad_preact, axis=0)
    grad_preact_low = grad_preact.astype(jnp.bfloat16)
    grad_fc1 = jnp.einsum("te,tf->ef", act_two, grad_preact_low, preferred_element_type=jnp.float32)
    grad_act_two = jnp.einsum(
        "tf,ef->te", grad_preact_low, fc1_low, preferred_element_type=jnp.float32
    )
    grad_mid_norm, grad_scale_two, grad_shift_two = norm_two_back(grad_act_two)
    grad_middle = grad_result + grad_mid_norm
    grad_out_shift = jnp.sum(grad_middle, axis=0)
    grad_middle_low = grad_middle.astype(jnp.bfloat16)
    grad_out = jnp.einsum(
        "te,td->ed", mixture_low, grad_middle_low, preferred_element_type=jnp.float32
    )
    grad_mixture = jnp.einsum(
        "td,ed->te", grad_middle_low, out_low, preferred_element_type=jnp.float32
    ).astype(jnp.bfloat16)
    grad_q, grad_k, grad_v = lax.map(
        partial(attend_backward, block_size=block_size, score_scale=score_scale),
        (
            query_heads,
            key_heads,
            value_heads,
            grad_mixture.reshape(head_shape),
            row_pictures,
            log_total,
        ),
    )
    grad_q = grad_q.reshape(-1, model_width)
    grad_k = grad_k.reshape(-1, model_width)
    grad_v = grad_v.reshape(-1, model_width)
    grad_query_shift = jnp.sum(grad_q, axis=0)
    grad_value_shift = jnp.sum(grad_v, axis=0)
    grad_projected = jnp.concatenate([grad_q, grad_k, grad_v], axis=1).astype(jnp.bfloat16)
    grad_qkv = jnp.einsum("te,tf->ef", act_one, grad_projected, preferred_element_type=jnp.float32)
    grad_act_one = jnp.einsum(
        "tf,ef->te", grad_projected, qkv_low, preferred_element_type=jnp.float32
    )
    grad_stream_norm, grad_scale_one, grad_shift_one = norm_one_back(grad_act_one)
    tokens_grad = (grad_middle + grad_stream_norm).astype(jnp.bfloat16)
    grad_vectors = jnp.stack(
        [
            grad_scale_one,
            grad_shift_one,
            grad_query_shift,
            grad_value_shift,
            grad_out_shift,
            grad_scale_two,
            grad_shift_two,
            grad_fc2_shift,
        ]
    )
    gradients = (grad_qkv, grad_out, grad_fc1, grad_fc2, grad_vectors, grad_fc1_shift)
    shard_count = lax.axis_size("shard")
    data_count = lax.axis_size("dp")
    ordered = [
        owner_major(entry, dim_number, shard_count, data_count)
        for entry, dim_number in zip(gradients, (0, 0, 0, 0, 1, 0))
    ]
    pieces = (
        lax.psum_scatter(ordered[0], ("dp", "shard"), scatter_dimension=0, tiled=True),
        lax.psum_scatter(ordered[1], ("dp", "shard"), scatter_dimension=0, tiled=True),
        lax.psum_scatter(ordered[2], ("dp", "shard"), scatter_dimension=0, tiled=True),
        lax.psum_scatter(ordered[3], ("dp", "shard"), scatter_dimension=0, tiled=True),
        lax.psum_scatter(ordered[4], ("dp", "shard"), scatter_dimension=1, tiled=True),
        lax.psum_scatter(ordered[5], ("dp", "shard"), scatter_dimension=0, tiled=True),
    )
    piece_squares = sum((jnp.sum(entry * entry) for entry in pieces))
    square_sum, stream_sums = lax.psum((piece_squares, stream_local), ("dp", "shard"))
    owner_grads = (
        lax.all_gather(pieces[0].astype(jnp.bfloat16), "dp", axis=0, tiled=True).astype(
            jnp.float32
        ),
        lax.all_gather(pieces[1].astype(jnp.bfloat16), "dp", axis=0, tiled=True).astype(
            jnp.float32
        ),
        lax.all_gather(pieces[2].astype(jnp.bfloat16), "dp", axis=0, tiled=True).astype(
            jnp.float32
        ),
        lax.all_gather(pieces[3].astype(jnp.bfloat16), "dp", axis=0, tiled=True).astype(
            jnp.float32
        ),
        lax.all_gather(pieces[4].astype(jnp.bfloat16), "dp", axis=1, tiled=True).astype(
            jnp.float32
        ),
        lax.all_gather(pieces[5].astype(jnp.bfloat16), "dp", axis=0, tiled=True).astype(
            jnp.float32
        ),
    )
    stream_rms = jnp.sqrt(stream_sums[:5] / (stream_sums[5] * model_width))
    clip_factor = CLIP_NORM / jnp.maximum(jnp.sqrt(square_sum), CLIP_NORM)
    correction = 1.0 - ADAM_BETA**STEP
    updated = []
    for number in range(6):
        clipped = owner_grads[number] * clip_factor
        first_moment = ADAM_BETA * moments[number][0] + (1.0 - ADAM_BETA) * clipped
        second_moment = ADAM_BETA * moments[number][1] + (1.0 - ADAM_BETA) * clipped * clipped
        change = first_moment / correction / (jnp.sqrt(second_moment / correction) + ADAM_EPS)
        if number < 4:
            change = change + WEIGHT_DECAY * masters[number]
        if number == 4:
            updated.append(LEARN_RATE * change)
        else:
            updated.append(masters[number] - LEARN_RATE * change)
    return (
        layer_out,
        tokens_grad,
        owner_grads[0],
        owner_grads[1],
        owner_grads[2],
        owner_grads[3],
        owner_grads[4],
        owner_grads[5],
        updated[0],
        updated[1],
        updated[2],
        updated[3],
        updated[4],
        updated[5],
        stream_rms,
    )


def solution(mesh):
    placed = (
        P(("dp", "shard"), None),
        P(("dp", "shard")),
        P(("dp", "shard"), None),
        P("shard", None),
        P("shard", None),
        P("shard", None),
        P("shard", None),
        P(None, "shard"),
        P("shard"),
        P(None, "shard", None),
        P(None, "shard", None),
        P(None, "shard", None),
        P(None, "shard", None),
        P(None, None, "shard"),
        P(None, "shard"),
    )
    return jax.shard_map(
        body,
        mesh=mesh,
        in_specs=placed,
        out_specs=(
            P(("dp", "shard"), None),
            P(("dp", "shard"), None),
            P("shard", None),
            P("shard", None),
            P("shard", None),
            P("shard", None),
            P(None, "shard"),
            P("shard"),
            P("shard", None),
            P("shard", None),
            P("shard", None),
            P("shard", None),
            P(None, "shard"),
            P("shard"),
            P(),
        ),
        check_vma=False,
    )
```

profile of v0, /device:TPU:0, one launch (start us, length us, event | category | flops | bytes accessed | tf_op | source)
XLA Modules:
  0.0 891.1 jit_solution(16528446712021270004)
XLA Ops:
  7.2 2.1 convert_element_type.126
  10.2 0.9 convert_element_type.135
  11.2 0.9 convert_element_type.139
  12.1 28.0 %all-gather.1 = bf16[8,1,384]{2,1,0:T(2,128)(2,1)S(1)} all-gather(bf16[1,1,384]{2,1,0:T(2,128)(2,1)S(1)} %reshape.262), channel_id=1, replica_groups=mesh['dp'=4,'shard'=8] {'shard'}, dimensions={0}, use_global_device_ids=true | all-gather | bytes 6912 | tf_op jit(solution)/shard_map/all_gather | solution.py:126
  40.2 26.4 %all-gather = bf16[8,96,8]{1,2,0:T(8,128)(2,1)S(1)} all-gather(bf16[1,96,8]{1,2,0:T(8,128)(2,1)S(1)} %convert_bitcast_fusion), channel_id=1, replica_groups=mesh['dp'=4,'shard'=8] {'shard'}, dimensions={0}, use_global_device_ids=true | all-gather | bytes 13824 | tf_op jit(solution)/shard_map/all_gather | solution.py:125
  68.7 10.3 %all-gather.8.cloned.1.call-done = bf16[768,2304]{1,0:T(8,128)(2,1)} async-done(((bf16[96,2304]{1,0:T(8,128)(2,1)}), bf16[768,2304]{1,0:T(8,128)(2,1)}) %all-gather.8.cloned.1.call-update) | async-done | bytes 3538960 | tf_op jit(solution)/shard_map/all_gather | solution.py:121
  79.1 4.1 fusion.102
  83.3 1.0 slice.140
  84.2 1.2 fusion.29
  85.7 1.7 copy.77
  87.4 1.4 copy.75
  88.8 2.1 fusion.12
  90.9 2.6 fusion
  93.5 2.0 copy-done
  95.5 4.5 fusion.35
  100.0 21.4 %all-gather.10.cloned.1.call-done = bf16[768,768]{1,0:T(8,128)(2,1)} async-done(((bf16[96,768]{1,0:T(8,128)(2,1)}), bf16[768,768]{1,0:T(8,128)(2,1)}) %all-gather.10.cloned.1.call-update) | async-done | bytes 1179664 | tf_op jit(solution)/shard_map/all_gather | solution.py:122
  121.4 3.6 fusion.113
  125.3 77.5 %all-gather.12.cloned.1.call-done = bf16[768,3072]{1,0:T(8,128)(2,1)} async-done(((bf16[96,3072]{1,0:T(8,128)(2,1)}), bf16[768,3072]{1,0:T(8,128)(2,1)}) %all-gather.12.cloned.1.call-update) | async-done | bytes 4718608 | tf_op jit(solution)/shard_map/all_gather | solution.py:123
  202.8 7.0 fusion.105
  209.8 73.6 %all-gather.14.cloned.1.call-done = bf16[3072,768]{1,0:T(8,128)(2,1)} async-done(((bf16[384,768]{1,0:T(8,128)(2,1)}), bf16[3072,768]{1,0:T(8,128)(2,1)}) %all-gather.14.cloned.1.call-update) | async-done | bytes 4718608 | tf_op jit(solution)/shard_map/all_gather | solution.py:124
  283.5 9.2 %fusion.110 = (f32[3072]{0:T(1024)S(1)}, bf16[512,3072]{1,0:T(8,128)(2,1)S(1)}) fusion(f32[512,3072]{1,0:T(8,128)} %fusion.105, f32[3072]{0:T(1024)S(1)} %bitcast.143, bf16[512,768]{1,0:T(8,128)(2,1)} %param.17, bf16[3072,768]{1,0:T(8,128)(2,1)} %all-gather.14.cloned.1.call-done), kind=kOutput, calls=%fused_computation.200 | convolution fusion | flops 2450519040 | bytes 14966784 | tf_op jit(solution)/shard_map/td,fd->tf/dot_general | solution.py:171
  292.8 2.7 fusion.33
  296.2 1.9 copy-done.40
  298.1 6.4 fusion.25
  305.2 1.2 copy-done.2
  306.4 1.7 convolution_convert_fusion
  308.1 2.3 copy.79
  310.4 2.8 convolution_bitcast_fusion
  313.2 1.6 copy.84
  314.8 13.6 %multiply_reduce_fusion = (f32[12,512]{1,0:T(8,128)S(1)}, f32[12,512,512]{1,2,0:T(8,128)}) fusion(f32[12,512]{1,0:T(8,128)S(1)} %log_add_fusion, f32[12,512,512]{1,2,0:T(8,128)} %copy-done, pred[512,512]{0,1:T(8,128)(4,1)S(1)} %broadcast_compare_fusion, bf16[512,12,64]{0,2,1:T(8,128)(2,1)} %bitcast.133, bf16[512,12,64]{0,2,1:T(8,128)(2,1)} %bitcast.132), kind=kOutput, calls=%fused_computation.1 | convolution fusion | flops 418375680 | bytes 27049984 | tf_op jit(solution)/shard_map/while/body/eval_jaxpr/qhd,khd->hqk/dot_general | solution.py:62
  328.5 7.5 multiply_convert_fusion
  336.0 2.0 multiply_convert_fusion.2
  338.0 2.3 bitcast_convert_fusion.1
  340.3 4.1 bitcast_convert_fusion
  344.5 2.3 fusion.54
  346.8 3.5 copy.83
  350.4 1.1 copy-done.15
  351.4 6.0 fusion.107
  357.4 4.7 copy.86
  362.8 4.8 fusion.31
  367.6 4.3 copy.85
  374.8 1.6 bitcast_reduce_fusion
  376.7 6.3 fusion.109
  384.5 1.7 convert_reduce_fusion.1
  386.8 39.2 %all-reduce.4 = (f32[8,768]{1,0:T(8,128)S(1)}, f32[3072]{0:T(1024)S(1)}) all-reduce(f32[8,768]{1,0:T(8,128)S(1)} %reshape.254, f32[3072]{0:T(1024)S(1)} %reshape.256), channel_id=6, replica_groups=mesh['dp'=4,'shard'=8] {'dp','shard'}, use_global_device_ids=true, to_apply=%region_23.24.clone | all-reduce | flops 9216 | bytes 73728
  426.1 5.4 all-gather.2
  431.9 4.0 stack.63
  437.2 7.5 all-reduce
  444.8 1.6 fusion.117
  446.4 5.5 all_gather.43
  451.8 84.9 %reduce-scatter.6.cloned.1.call-done = f32[24,2304]{1,0:T(8,128)} async-done(((f32[768,2304]{1,0:T(8,128)}), f32[24,2304]{1,0:T(8,128)}) %reduce-scatter.6.cloned.1.call-update) | async-done | bytes 221200 | tf_op jit(solution)/shard_map/reduce_scatter | solution.py:232
  536.7 1.7 fusion.116
  539.7 6.6 all_gather.42
  546.3 130.9 %reduce-scatter.12.cloned.1.call-done = f32[96,768]{1,0:T(8,128)} async-done(((f32[3072,768]{1,0:T(8,128)}), f32[96,768]{1,0:T(8,128)}) %reduce-scatter.12.cloned.1.call-update) | async-done | bytes 294928 | tf_op jit(solution)/shard_map/reduce_scatter | solution.py:235
  677.2 1.7 fusion.114
  679.0 7.7 all_gather.45
  686.7 132.2 %reduce-scatter.10.cloned.1.call-done = f32[24,3072]{1,0:T(8,128)} async-done(((f32[768,3072]{1,0:T(8,128)}), f32[24,3072]{1,0:T(8,128)}) %reduce-scatter.10.cloned.1.call-update) | async-done | bytes 294928 | tf_op jit(solution)/shard_map/reduce_scatter | solution.py:234
  819.0 1.7 fusion.115
  823.3 7.5 all_gather.44
  830.8 39.3 %all-reduce.3 = (f32[]{:T(128)}, f32[6]{0:T(128)S(1)}) all-reduce(f32[]{:T(128)S(6)} %add.269, f32[6]{0:T(128)S(1)} %stack.63), channel_id=1, replica_groups=mesh['dp'=4,'shard'=8] {'dp','shard'}, use_global_device_ids=true, to_apply=%region_32.33 | all-reduce | flops 7 | bytes 56 | tf_op jit(solution)/shard_map/psum | solution.py:240
  873.2 2.1 fusion.73
  875.3 3.5 fusion.60
  878.7 2.3 fusion.49
  881.1 2.3 fusion.40
  (166 shorter events, 14.6 us)
Async XLA Ops:
  7.2 2.2 copy-start.19
  7.2 3.0 copy-start.9
  7.2 71.9 %all-gather.8.cloned.1.call-start = ((), (), s32[]{:S(2)}) async-start(), calls=%async_computation.4 | async-start | bytes 3981312 | tf_op jit(solution)/shard_map/all_gather | solution.py:121
  9.4 1.8 copy-start.7
  9.4 112.0 %all-gather.10.cloned.1.call-start = ((), (), s32[]{:S(2)}) async-start(), calls=%async_computation.5 | async-start | bytes 1327104 | tf_op jit(solution)/shard_map/all_gather | solution.py:122
  10.1 192.7 %all-gather.12.cloned.1.call-start = ((), (), s32[]{:S(2)}) async-start(), calls=%async_computation.6 | async-start | bytes 5308416 | tf_op jit(solution)/shard_map/all_gather | solution.py:123
  11.1 1.0 copy-start.26
  11.1 29.1 %copy-start.32 = (f32[8,96]{1,0:T(8,128)S(1)}, f32[8,96]{1,0:T(8,128)}, u32[]{:S(2)}) copy-start(f32[8,96]{1,0:T(8,128)} %param.22) | copy-start | bytes 9220
  11.1 56.3 %copy-start.1 = (bf16[512,768]{1,0:T(8,128)(2,1)S(1)}, bf16[512,768]{1,0:T(8,128)(2,1)}, u32[]{:S(2)}) copy-start(bf16[512,768]{1,0:T(8,128)(2,1)} %param.15) | copy-start | bytes 2359300
  11.1 272.4 %all-gather.14.cloned.1.call-start = ((), (), s32[]{:S(2)}) async-start(), calls=%async_computation.7 | async-start | bytes 5308416 | tf_op jit(solution)/shard_map/all_gather | solution.py:124
  12.0 55.9 %copy-start.23 = (s32[512]{0:T(512)S(1)}, s32[512]{0:T(512)}, u32[]{:S(2)}) copy-start(s32[512]{0:T(512)} %param.16) | copy-start | bytes 6148
  12.1 432.7 %reduce-scatter.8.cloned.1.call-start = ((), (), s32[]{:S(2)}) async-start(), calls=%async_computation.9 | async-start | bytes 2433024 | tf_op jit(solution)/shard_map/reduce_scatter | solution.py:233
  67.4 15.9 %copy-start.29 = (f32[768]{0:T(1024)}, f32[768]{0:T(1024)S(1)}, u32[]{:S(2)}) copy-start(f32[768]{0:T(1024)S(1)} %get-tuple-element.87) | copy-start | bytes 9220
  85.7 3.2 copy-start.5
  88.8 4.7 copy-start.12
  90.9 4.6 copy-start
  283.5 9.2 %copy-start.36 = (bf16[768,3072]{1,0:T(8,128)(2,1)S(1)}, bf16[768,3072]{1,0:T(8,128)(2,1)}, u32[]{:S(2)}) copy-start(bf16[768,3072]{1,0:T(8,128)(2,1)} %all-gather.12.cloned.1.call-done) | copy-start | bytes 14155780
  292.7 2.7 copy-start.41
  292.7 2.7 copy-start.31
  292.7 2.7 copy-start.34
  292.7 3.5 copy-start.37
  292.8 5.3 copy-start.40
  304.5 1.9 copy-start.14
  304.5 1.9 copy-start.21
  305.1 1.2 copy-start.2
  314.8 222.0 %reduce-scatter.6.cloned.1.call-start = ((), (), s32[]{:S(2)}) async-start(), calls=%async_computation.8 | async-start | bytes 7299072 | tf_op jit(solution)/shard_map/reduce_scatter | solution.py:232
  314.8 13.6 %slice-start = ((s8[12582912]{0:T(1024)(128)(4,1)}), s8[4194304]{0:T(1024)(128)(4,1)S(1)}, s32[]{:S(2)}) async-start(s8[12582912]{0:T(1024)(128)(4,1)} %bitcast.116), calls=%async_computation.12 | async-start | bytes 8388608
  314.8 13.6 %slice-start.1 = ((s8[12582912]{0:T(1024)(128)(4,1)}), s8[4194304]{0:T(1024)(128)(4,1)S(1)}, s32[]{:S(2)}) async-start(s8[12582912]{0:T(1024)(128)(4,1)} %bitcast.116), calls=%async_computation.13 | async-start | bytes 8388608
  314.8 13.6 %slice-start.2 = ((s8[12582912]{0:T(1024)(128)(4,1)}), s8[4194304]{0:T(1024)(128)(4,1)S(1)}, s32[]{:S(2)}) async-start(s8[12582912]{0:T(1024)(128)(4,1)} %bitcast.116), calls=%async_computation.14 | async-start | bytes 8388608
  328.5 7.5 copy-start.6
  338.0 6.5 copy-start.22
  338.0 2.3 copy-start.13
  340.3 4.1 copy-start.16
  340.3 4.1 copy-start.30
  344.5 2.4 copy-start.38
  350.3 1.1 copy-start.15
  350.3 326.9 %reduce-scatter.12.cloned.1.call-start = ((), (), s32[]{:S(2)}) async-start(), calls=%async_computation.11 | async-start | bytes 9732096 | tf_op jit(solution)/shard_map/reduce_scatter | solution.py:235
  362.1 0.7 copy-start.28
  362.1 456.9 %reduce-scatter.10.cloned.1.call-start = ((), (), s32[]{:S(2)}) async-start(), calls=%async_computation.10 | async-start | bytes 9732096 | tf_op jit(solution)/shard_map/reduce_scatter | solution.py:234
  371.9 0.7 copy-start.39
  371.9 2.5 copy-start.33
  371.9 4.5 copy-start.4
  374.7 2.0 copy-start.35
  383.1 1.4 copy-start.3
  431.6 440.9 %copy-start.24 = (f32[96,8]{0,1:T(8,128)}, f32[96,8]{0,1:T(8,128)S(1)}, u32[]{:S(2)}) copy-start(f32[96,8]{0,1:T(8,128)S(1)} %reshape.270) | copy-start | bytes 9220
  451.8 420.7 %copy-start.25 = (f32[2,8,96]{2,1,0:T(8,128)S(1)}, f32[2,8,96]{2,1,0:T(8,128)}, u32[]{:S(2)}) copy-start(f32[2,8,96]{2,1,0:T(8,128)} %param.28) | copy-start | bytes 18436
  451.8 421.4 %copy-start.20 = (f32[96,768]{1,0:T(8,128)S(1)}, f32[96,768]{1,0:T(8,128)}, u32[]{:S(2)}) copy-start(f32[96,768]{1,0:T(8,128)} %param.19) | copy-start | bytes 884740
  686.7 188.5 %copy-start.11 = (f32[96,2304]{1,0:T(8,128)S(1)}, f32[96,2304]{1,0:T(8,128)}, u32[]{:S(2)}) copy-start(f32[96,2304]{1,0:T(8,128)} %param.18) | copy-start | bytes 2654212
  875.3 3.5 copy-start.8
  875.3 3.5 copy-start.17
  878.7 2.3 copy-start.10
  878.7 2.3 copy-start.18
  881.1 2.3 copy-start.27
Sparse Core Ops, SparseCore 0:
  10.8 68.2 all-gather.7
  81.8 39.4 all-gather.9
  124.1 78.6 all-gather.11
  205.4 78.0 all-gather.13
  314.9 97.3 reduce-scatter.7
  418.7 117.9 reduce-scatter.5
  542.6 134.5 reduce-scatter.11
  684.1 134.7 reduce-scatter.9
where the time goes:
time: 899 us; the launch traced here: 891 us
  waiting for transfers between devices  531 us (59%)
  blocking collectives  173 us (19%)
  matrix products  85.7 us (10%)
  other arithmetic  43 us (5%)
  local copies, waits for them, and re-layouts  36.6 us (4%)
  between operations  20.9 us (2%)
    reduce_scatter x1, waiting for transfers between devices, body(): lax.psum_scatter(ordered[2], ('dp', 'shard'), scatter_dimension=0, tiled=...  132 us
    reduce_scatter x1, waiting for transfers between devices, body(): lax.psum_scatter(ordered[3], ('dp', 'shard'), scatter_dimension=0, tiled=...  131 us
    reduce_scatter x1, waiting for transfers between devices, body(): lax.psum_scatter(ordered[0], ('dp', 'shard'), scatter_dimension=0, tiled=...  84.9 us
    all_gather x1, waiting for transfers between devices, body(): lax.all_gather(w_fc1.astype(jnp.bfloat16), 'shard', axis=0, tiled=True)  77.5 us
    all_gather x1, waiting for transfers between devices, body(): lax.all_gather(w_fc2.astype(jnp.bfloat16), 'shard', axis=0, tiled=True)  73.6 us
    unnamed x2, blocking collectives  46.8 us
    psum x1, blocking collectives, body(): lax.psum((piece_squares, stream_local), ('dp', 'shard'))  39.3 us
    all_gather x1, blocking collectives, body(): lax.all_gather(fc1_bias.astype(jnp.bfloat16), 'shard', axis=0, tiled=True)  28 us
  transfers between devices with their start and end apart: 8, of which 7 were waited for; matrix products, arithmetic and copies ran while one was open for 13% of the time, Pallas kernels for 0%

commit v1 on v0

v1 whole, which is shorter than its diff:
```python
from functools import partial

import jax
import jax.numpy as jnp
from jax import lax
from jax.experimental import pallas as pl
from jax.experimental.pallas import tpu as pltpu
from jax.sharding import PartitionSpec as P

HEADS = 12
HEAD_DIM = 64
ROW = 512
STEP = 2

NORM_EPS = 1e-06
ADAM_BETA = 0.5
LEARN_RATE = 0.03
WEIGHT_DECAY = 0.1
ADAM_EPS = 1e-08
CLIP_NORM = 1.0
MASKED = -1e30
GELU_SCALE = 0.7978845608028654
GELU_CUBE = 0.044715

LOW = jnp.bfloat16
WIDE = jnp.float32


def swap(entry, axis, mask, name="sums"):
    count = lax.axis_size(axis)
    with jax.named_scope(name + "_" + axis + str(mask)):
        return lax.ppermute(entry, axis, [(place, place ^ mask) for place in range(count)])


def in_vmem():
    return pl.BlockSpec(memory_space=pltpu.VMEM)


def in_hbm():
    return pl.BlockSpec(memory_space=pltpu.HBM)


def hbm(entries):
    return [pltpu.with_memory_space_constraint(entry, pltpu.HBM) for entry in entries]


def in_smem():
    return pl.BlockSpec(memory_space=pltpu.SMEM)


def shape(dims, kind=LOW):
    return jax.ShapeDtypeStruct(dims, kind)


def cost(flops, moved):
    return pl.CostEstimate(flops=1, bytes_accessed=1, transcendentals=0)


def kernel_params(mib):
    return pltpu.CompilerParams(vmem_limit_bytes=mib * 2**20)


def dot(left, right):
    return jnp.dot(left, right, preferred_element_type=WIDE)


def dot_t(left, right):
    return lax.dot_general(left, right, (((1,), (1,)), ((), ())), preferred_element_type=WIDE)


def normalize(entries):
    center = entries - jnp.mean(entries, axis=-1, keepdims=True)
    scale = lax.rsqrt(jnp.mean(center * center, axis=-1, keepdims=True) + NORM_EPS)
    return center * scale, scale


def normalize_back(grad, normed, scale):
    inner = jnp.mean(grad * normed, axis=-1, keepdims=True)
    return scale * (grad - jnp.mean(grad, axis=-1, keepdims=True) - normed * inner)


def column_sum(entries):
    return jnp.sum(entries, axis=0, keepdims=True)


def own_pieces_kernel(place_ref, *refs):
    sources, vectors_ref, shift_ref = refs[:4], refs[4], refs[5]
    qkv_ref, mid_ref, fc2_ref = refs[6:9]
    scratch, sem = refs[9:13], refs[13]
    core, plane = place_ref[1], place_ref[2]
    copies = []
    for source, held in zip(sources, scratch):
        slots, rows, lanes = held.shape
        parts = (plane, 2) if slots == 2 else (0, 1, 2)
        column = pl.multiple_of(core * lanes, 128)
        for slot, part in enumerate(parts):
            start = pl.multiple_of(part * rows, rows)
            copies.append(
                pltpu.make_async_copy(
                    source.at[pl.ds(start, rows), pl.ds(column, lanes)],
                    held.at[slot],
                    sem.at[len(copies)],
                )
            )
    for copy in copies:
        copy.start()
    for copy in copies:
        copy.wait()
    qkv, out, fc1, fc2 = scratch
    width = qkv.shape[2]
    qkv_ref[:, :, :width] = qkv[...].astype(LOW)
    qkv_ref[:, :, width:] = jnp.zeros((2, qkv.shape[1], 128), LOW)
    qkv_ref[1, 0:8, width : width + vectors_ref.shape[1]] = vectors_ref[...].astype(LOW)
    qkv_ref[1, 8 : 8 + shift_ref.shape[0], width:] = shift_ref[...].astype(LOW)
    width = out.shape[2]
    mid_ref[:, :, :width] = out[...].astype(LOW)
    mid_ref[:, :, width:] = fc1[...].astype(LOW)
    fc2_ref[...] = fc2[...].astype(LOW)


def own_pieces(place, w_qkv, w_out, w_fc1, w_fc2, vectors, fc1_bias):
    weights = (w_qkv, w_out, w_fc1, w_fc2)
    dims = [
        (slots, entry.shape[0] // 3, entry.shape[1] // 2)
        for slots, entry in zip((2, 2, 2, 3), weights)
    ]
    rows = dims[0][1]
    return pl.pallas_call(
        own_pieces_kernel,
        out_shape=[
            shape((2, rows, dims[0][2] + 128)),
            shape((2, rows, dims[1][2] + dims[2][2])),
            shape(dims[3]),
        ],
        in_specs=[in_smem()] + [in_hbm()] * 4 + [in_vmem()] * 2,
        out_specs=[in_vmem()] * 3,
        scratch_shapes=[pltpu.VMEM(entry, WIDE) for entry in dims] + [pltpu.SemaphoreType.DMA((9,))],
        compiler_params=kernel_params(8),
    )(place, *hbm(weights), vectors, fc1_bias.reshape(-1, 128))


def after(entry, *others):
    return lax.optimization_barrier((entry, *others))[0]


def sync(*entries):
    leaves, tree = jax.tree.flatten(entries)
    return jax.tree.unflatten(tree, lax.optimization_barrier(leaves))


def gather_z(own, name):
    return [own] + [swap(own, "shard", mask, name) for mask in (2, 4, 6)]


def gather_x(near, name):
    return swap(near, "shard", 1, name)


def gather_y(near, far, name, lanes=None):
    return swap(jnp.concatenate([near[0, :, :, :lanes], far[0, :, :, :lanes]]), "dp", 2, name)


def gather_core(entry, name):
    return swap(entry, "dp", 1, name)


def load_weight(place_ref, pieces, first, width, full, sem):
    shard, core, plane = place_ref[0], place_ref[1], place_ref[2]
    rows = pieces[0].shape[2]
    lanes = pl.ds(first, width)

    def put(source, owner, part, which):
        row = pl.multiple_of((owner * 3 + part) * rows, rows)
        column = pl.multiple_of(which * width, 128)
        pltpu.make_async_copy(source, full.at[pl.ds(row, rows), pl.ds(column, width)], sem).start()

    count = len(pieces) // 2
    for which, half in ((core, pieces[:count]), (1 - core, pieces[count:])):
        for flip in range(2):
            for step in range(4):
                owner = shard ^ (2 * step + flip)
                if count == 2:
                    for part in range(3):
                        put(half[flip].at[part, step, :, lanes], owner, part, which)
                else:
                    put(half[flip].at[0, step, :, lanes], owner, plane, which)
                    put(half[flip].at[1, step, :, lanes], owner, 2, which)
                    put(half[2].at[4 * flip + step, :, lanes], owner, 1 - plane, which)
    return pltpu.make_async_copy(full, full, sem)


def gather_vectors(place_ref, near, far, held, sem, vec_ref, shift_ref):
    lane = near.shape[3] - 128
    owned = vec_ref.shape[1] // 8
    for flip, ref in ((0, near), (1, far)):
        for step in range(4):
            source = ref.at[1, step, pl.ds(0, 16), pl.ds(lane, 128)]
            pltpu.make_async_copy(source, held.at[4 * flip + step], sem).start()
    pltpu.make_async_copy(held, held, sem).wait()
    source = lax.broadcasted_iota(jnp.int32, (128, vec_ref.shape[1]), 0)
    target = lax.broadcasted_iota(jnp.int32, (128, vec_ref.shape[1]), 1)
    rows = jnp.zeros((16, vec_ref.shape[1]), WIDE)
    count = shift_ref.shape[1] // (8 * 128)
    for order in range(8):
        owner = place_ref[0] ^ (2 * (order % 4) + order // 4)
        move = (target == source + owner * owned) & (source < owned)
        rows = rows + dot(held[order], move.astype(WIDE).astype(LOW))
        for row in range(count):
            start = pl.multiple_of((owner * count + row) * 128, 128)
            shift_ref[0:1, pl.ds(start, 128)] = held[order, 8 + row : 9 + row, :].astype(WIDE)
    vec_ref[...] = rows[0:8]


def attention_kernel(place_ref, stream_ref, ids_column_ref, ids_row_ref, *refs):
    pieces = refs[:6]
    vec_ref, shift_ref, a1_t_ref, mix_ref, mix_t_ref, qkv_out, prob_out = refs[6:13]
    weight, qkv_ref, prob, bias, v_t, weight_sem, vec_held, vec_sem, out_sem = refs[13:]
    width = mix_ref.shape[1]
    pairs = width // 128
    loading = load_weight(place_ref, pieces, 0, weight.shape[1] // 2, weight, weight_sem)
    gather_vectors(place_ref, *pieces[:2], vec_held, vec_sem, vec_ref, shift_ref)
    normed, _ = normalize(stream_ref[...].astype(WIDE))
    a1 = (normed * vec_ref[0:1, :] + vec_ref[1:2, :]).astype(LOW)
    a1_t_ref[...] = a1.T
    bias[...] = jnp.where(ids_column_ref[...] == ids_row_ref[...], 0.0, MASKED)
    loading.wait()
    queries = dot(a1, weight[:, :width]) + vec_ref[2:3, :]
    qkv_ref[:, :width] = queries.astype(LOW)
    qkv_ref[:, width : 2 * width] = dot(a1, weight[:, width : 2 * width]).astype(LOW)
    values = (dot(a1, weight[:, 2 * width :]) + vec_ref[3:4, :]).astype(LOW)
    qkv_ref[:, 2 * width :] = values
    qkv_copy = pltpu.make_async_copy(qkv_ref, qkv_out, out_sem.at[pairs])
    qkv_copy.start()
    v_t[...] = values.T

    def out_copy(pair):
        heads = pl.ds(2 * pair, 2)
        return pltpu.make_async_copy(prob.at[heads], prob_out.at[heads], out_sem.at[pair])

    left = lax.broadcasted_iota(jnp.int32, (ROW, 128), 1) < HEAD_DIM

    @pl.loop(0, pairs)
    def _(pair):
        lane = pl.multiple_of(pair * 128, 128)
        scaled = qkv_ref[:, pl.ds(lane, 128)] * HEAD_DIM**-0.5
        keys = qkv_ref[:, pl.ds(width + lane, 128)]
        for half in range(2):
            key_half = jnp.where(left == (half == 0), keys, jnp.zeros_like(keys))
            v_rows = pl.ds(pl.multiple_of(lane + half * HEAD_DIM, HEAD_DIM), HEAD_DIM)
            for block in range(2):
                rows = slice(block * 256, block * 256 + 256)
                scores = dot_t(key_half, scaled[rows]) + bias[:, rows]
                weights = jnp.exp(scores - jnp.max(scores, axis=0, keepdims=True))
                weights = weights * (1.0 / jnp.sum(weights, axis=0, keepdims=True))
                low = weights.astype(LOW)
                prob[2 * pair + half, :, rows] = low
                mix_t_ref[v_rows, rows] = dot(v_t[v_rows, :], low).astype(LOW)
        out_copy(pair).start()

    mix_ref[...] = mix_t_ref[...].T
    qkv_copy.wait()

    @pl.loop(0, pairs)
    def _(pair):
        out_copy(pair).wait()


def attention(place, stream, ids, hidden, pieces):
    width = stream.shape[1]
    return pl.pallas_call(
        attention_kernel,
        out_shape=[
            shape((8, width), WIDE),
            shape((1, hidden), WIDE),
            shape((width, ROW)),
            shape((ROW, width)),
            shape((width, ROW)),
            pltpu.HBM((ROW, 3 * width), LOW),
            pltpu.HBM((HEADS, ROW, ROW), LOW),
        ],
        in_specs=[in_smem()] + [in_vmem()] * 3 + [in_hbm()] * 6,
        out_specs=[in_vmem()] * 5 + [in_hbm()] * 2,
        scratch_shapes=[
            pltpu.VMEM((width, 3 * width), LOW),
            pltpu.VMEM((ROW, 3 * width), LOW),
            pltpu.VMEM((HEADS, ROW, ROW), LOW),
            pltpu.VMEM((ROW, ROW), WIDE),
            pltpu.VMEM((width, ROW), LOW),
            pltpu.SemaphoreType.DMA,
            pltpu.VMEM((8, 16, 128), LOW),
            pltpu.SemaphoreType.DMA,
            pltpu.SemaphoreType.DMA((HEADS // 2 + 1,)),
        ],
        compiler_params=kernel_params(22),
        cost_estimate=cost(12e9, 24e6),
    )(place, stream, ids.reshape(ROW, 1), ids.reshape(1, ROW), *hbm(pieces))


def hidden_kernel(place_ref, tokens_ref, mix_ref, valid_ref, vec_ref, bias_ref, *refs):
    pieces = refs[:6]
    mid_ref, a2_t_ref, act_ref, act_t_ref, slope_ref, sums_ref, w_out, w_fc1 = refs[6:14]
    out_sem, fc1_sem = refs[14:]
    width = tokens_ref.shape[1]
    hidden = bias_ref.shape[1]
    out_ready = load_weight(place_ref, pieces, 0, width // 2, w_out, out_sem)
    fc1_ready = load_weight(place_ref, pieces, width // 2, hidden // 2, w_fc1, fc1_sem)
    stream = tokens_ref[...].astype(WIDE)
    valid = valid_ref[...]
    out_ready.wait()
    branch = dot(mix_ref[...], w_out[...]) + vec_ref[4:5, :]
    middle = stream + branch
    mid_ref[...] = middle
    sums_ref[0:1, :] = column_sum(valid * stream * stream)
    sums_ref[1:2, :] = column_sum(valid * branch * branch)
    sums_ref[2:3, :] = column_sum(valid * middle * middle)
    sums_ref[3:8, :] = jnp.zeros((5, width), WIDE)
    normed, _ = normalize(middle)
    a2 = (normed * vec_ref[5:6, :] + vec_ref[6:7, :]).astype(LOW)
    a2_t_ref[...] = a2.T
    fc1_ready.wait()
    step = 512
    for first in range(0, hidden, step):
        lanes = slice(first, first + step)
        pre = dot(a2, w_fc1[:, lanes]) + bias_ref[:, lanes]
        square = pre * pre
        turn = jnp.tanh(GELU_SCALE * (pre + GELU_CUBE * (square * pre)))
        half = 0.5 * (1.0 + turn)
        act = (pre * half).astype(LOW)
        act_ref[:, lanes] = act
        act_t_ref[lanes, :] = act.T
        bend = (1.0 - turn * turn) * (GELU_SCALE + 3.0 * GELU_SCALE * GELU_CUBE * square)
        slope_ref[:, lanes] = (half + 0.5 * pre * bend).astype(LOW)


def hidden_layer(place, tokens, mix, valid, vec, bias, pieces):
    width, hidden = tokens.shape[1], bias.shape[1]
    return pl.pallas_call(
        hidden_kernel,
        out_shape=[
            shape((ROW, width), WIDE),
            shape((width, ROW)),
            shape((ROW, hidden)),
            shape((hidden, ROW)),
            shape((ROW, hidden)),
            shape((8, width), WIDE),
            shape((width, width)),
            shape((width, hidden)),
        ],
        in_specs=[in_smem()] + [in_vmem()] * 5 + [in_hbm()] * 6,
        out_specs=[in_vmem()] * 8,
        scratch_shapes=[
            pltpu.SemaphoreType.DMA,
            pltpu.SemaphoreType.DMA,
        ],
        compiler_params=kernel_params(16),
        cost_estimate=cost(10e9, 20e6),
    )(place, tokens, mix, valid, vec, bias, *hbm(pieces))


def hidden_back_kernel(place_ref, cot_ref, slope_ref, *refs):
    pieces = refs[:4]
    d_pre_ref, shift_ref, w_fc2, sem = refs[4:]
    hidden = slope_ref.shape[1]
    loading = load_weight(place_ref, pieces, 0, w_fc2.shape[1] // 2, w_fc2, sem)
    cot = cot_ref[...]
    loading.wait()
    step = 512
    for first in range(0, hidden, step):
        lanes = slice(first, first + step)
        d_pre = dot_t(cot, w_fc2[lanes, :]) * slope_ref[:, lanes].astype(WIDE)
        shift_ref[:, lanes] = column_sum(d_pre)
        d_pre_ref[:, lanes] = d_pre.astype(LOW)


def hidden_back(place, cot, slope, pieces):
    width, hidden = cot.shape[1], slope.shape[1]
    return pl.pallas_call(
        hidden_back_kernel,
        out_shape=[shape((ROW, hidden)), shape((1, hidden), WIDE), shape((hidden, width))],
        in_specs=[in_smem()] + [in_vmem()] * 2 + [in_hbm()] * 4,
        out_specs=[in_vmem()] * 3,
        scratch_shapes=[pltpu.SemaphoreType.DMA],
        compiler_params=kernel_params(18),
        cost_estimate=cost(3e9, 14e6),
    )(place, cot, slope, *hbm(pieces))


def middle_kernel(mid_ref, act_ref, d_pre_ref, cot_ref, valid_ref, vec_ref, *refs):
    w_out, w_fc1, w_fc2 = refs[:3]
    layer_ref, d_mid_ref, d_mid_low_ref, d_mix_ref, sums_ref = refs[3:]
    middle = mid_ref[...]
    valid = valid_ref[...]
    mlp = dot(act_ref[...], w_fc2[...]) + vec_ref[7:8, :]
    result = middle + mlp
    layer_ref[...] = result.astype(LOW)
    sums_ref[4:5, :] = column_sum(valid * mlp * mlp)
    sums_ref[5:6, :] = column_sum(valid * result * result)
    sums_ref[6:8, :] = jnp.zeros((2, mid_ref.shape[1]), WIDE)
    d_a2 = dot_t(d_pre_ref[...], w_fc1[...])
    normed, scale = normalize(middle)
    dy = cot_ref[...].astype(WIDE)
    d_mid = dy + normalize_back(d_a2 * vec_ref[5:6, :], normed, scale)
    d_mid_ref[...] = d_mid
    low = d_mid.astype(LOW)
    d_mid_low_ref[...] = low
    sums_ref[0:1, :] = column_sum(d_mid)
    sums_ref[1:2, :] = column_sum(d_a2 * normed)
    sums_ref[2:3, :] = column_sum(d_a2)
    sums_ref[3:4, :] = column_sum(dy)
    d_mix_ref[...] = dot_t(low, w_out[...]).astype(LOW)


def middle_layer(mid, act, d_pre, cot, valid, vec, w_out, w_fc1, w_fc2):
    width = mid.shape[1]
    return pl.pallas_call(
        middle_kernel,
        out_shape=[
            shape((ROW, width)),
            shape((ROW, width), WIDE),
            shape((ROW, width)),
            shape((ROW, width)),
            shape((8, width), WIDE),
        ],
        in_specs=[in_vmem()] * 9,
        out_specs=[in_vmem()] * 5,
        compiler_params=kernel_params(20),
        cost_estimate=cost(14e9, 30e6),
    )(mid, act, d_pre, cot, valid, vec, w_out, w_fc1, w_fc2)


def attention_back_kernel(qkv_ref, mix_t_ref, d_mix_ref, prob_in, d_proj_ref, sums_ref, *rest):
    k_t, d_mix_t, d_q_t, prob, sem = rest
    width = mix_t_ref.shape[0]
    pairs = width // 128

    def in_copy(pair):
        heads = pl.ds(2 * pair, 2)
        return pltpu.make_async_copy(prob_in.at[heads], prob.at[heads], sem.at[pair])

    @pl.loop(0, pairs)
    def _(pair):
        in_copy(pair).start()


    k_t[...] = qkv_ref[:, width : 2 * width].T
    d_mix_t[...] = d_mix_ref[...].T
    left = lax.broadcasted_iota(jnp.int32, (ROW, 128), 1) < HEAD_DIM

    @pl.loop(0, pairs)
    def _(pair):
        lane = pl.multiple_of(pair * 128, 128)
        queries = qkv_ref[:, pl.ds(lane, 128)]
        values = qkv_ref[:, pl.ds(2 * width + lane, 128)]
        d_mix = d_mix_ref[:, pl.ds(lane, 128)]
        in_copy(pair).wait()
        d_keys, d_values = [], []
        for half in range(2):
            rows = pl.ds(pl.multiple_of(lane + half * HEAD_DIM, HEAD_DIM), HEAD_DIM)
            inner = column_sum(mix_t_ref[rows, :].astype(WIDE) * d_mix_t[rows, :].astype(WIDE))
            value_half = jnp.where(left == (half == 0), values, jnp.zeros_like(values))
            d_key, d_value = [], []
            for block in range(2):
                lanes = slice(block * 256, block * 256 + 256)
                low = prob[2 * pair + half, :, lanes]
                d_prob = dot_t(value_half, d_mix[lanes])
                d_score = (low.astype(WIDE) * (d_prob - inner[:, lanes])).astype(LOW)
                d_key.append(dot(d_score, queries[lanes]))
                d_value.append(dot(low, d_mix[lanes]))
                d_q_t[rows, lanes] = dot(k_t[rows, :], d_score)
            d_keys.append(d_key[0] + d_key[1])
            d_values.append(d_value[0] + d_value[1])
        d_k = jnp.where(left, d_keys[0], d_keys[1]) * HEAD_DIM**-0.5
        d_v = jnp.where(left, d_values[0], d_values[1])
        d_proj_ref[:, pl.ds(width + lane, 128)] = d_k.astype(LOW)
        d_proj_ref[:, pl.ds(2 * width + lane, 128)] = d_v.astype(LOW)
        sums_ref[1:2, pl.ds(lane, 128)] = column_sum(d_v)

    d_q = d_q_t[...].T * HEAD_DIM**-0.5
    d_proj_ref[:, :width] = d_q.astype(LOW)
    sums_ref[0:1, :] = column_sum(d_q)
    sums_ref[2:8, :] = jnp.zeros((6, width), WIDE)


def attention_back(qkv, mix_t, d_mix, prob):
    width = mix_t.shape[0]
    heads = prob.shape[0]
    return pl.pallas_call(
        attention_back_kernel,
        out_shape=[shape((ROW, 3 * width)), shape((8, width), WIDE)],
        in_specs=[in_vmem()] * 3 + [in_hbm()],
        out_specs=[in_vmem()] * 2,
        scratch_shapes=[
            pltpu.VMEM((width, ROW), LOW),
            pltpu.VMEM((width, ROW), LOW),
            pltpu.VMEM((width, ROW), WIDE),
            pltpu.VMEM((heads, ROW, ROW), LOW),
            pltpu.SemaphoreType.DMA((heads // 2,)),
        ],
        compiler_params=kernel_params(20),
        cost_estimate=cost(1.2e9 * heads, 2e6 * heads),
    )(qkv, mix_t, d_mix, *hbm([prob]))


def first_norm_kernel(place_ref, tokens_ref, d_proj_ref, d_mid_ref, vec_ref, *refs):
    pieces = refs[:6]
    grad_ref, sums_ref, weight, sem = refs[6:]
    loading = load_weight(place_ref, pieces, 0, weight.shape[1] // 2, weight, sem)
    normed, scale = normalize(tokens_ref[...].astype(WIDE))
    loading.wait()
    d_a1 = dot_t(d_proj_ref[...], weight[...])
    d_in = normalize_back(d_a1 * vec_ref[0:1, :], normed, scale)
    grad_ref[...] = (d_mid_ref[...] + d_in).astype(LOW)
    sums_ref[0:1, :] = column_sum(d_a1 * normed)
    sums_ref[1:2, :] = column_sum(d_a1)
    sums_ref[2:8, :] = jnp.zeros((6, d_a1.shape[1]), WIDE)


def first_norm_back(place, tokens, d_proj, d_mid, vec, pieces):
    width = tokens.shape[1]
    return pl.pallas_call(
        first_norm_kernel,
        out_shape=[shape((ROW, width)), shape((8, width), WIDE)],
        in_specs=[in_smem()] + [in_vmem()] * 4 + [in_hbm()] * 6,
        out_specs=[in_vmem()] * 2,
        scratch_shapes=[pltpu.VMEM((width, d_proj.shape[1]), LOW), pltpu.SemaphoreType.DMA],
        compiler_params=kernel_params(16),
        cost_estimate=pl.CostEstimate(flops=4_000_000_000, bytes_accessed=1, transcendentals=0),
    )(place, tokens, d_proj, d_mid, vec, *hbm(pieces))


def product_half(left_refs, right_ref, which, sums, first):
    half = right_ref.shape[1] // 2
    row = 0
    for left_ref in left_refs:
        count = left_ref.shape[0]
        for start in range(0, half, 384):
            lane = pl.multiple_of(which * half + start, 128)
            sums[row : row + count, first + start : first + start + 384] = dot(
                left_ref[...], right_ref[:, pl.ds(lane, 384)]
            )
        row += count


def products(groups, refs, which, sums):
    first = 0
    for count in groups:
        product_half(refs[:count], refs[count], which, sums, first)
        first += refs[count].shape[1] // 2
        refs = refs[count + 1 :]


def give_kernel(groups, place_ref, *refs):
    out_ref, sums = refs[-2:]
    shard, core = place_ref[0], place_ref[1]
    products(groups, refs[:-2], 1 - core, sums)
    rows = out_ref.shape[2]
    for order in range(8):
        owner = shard ^ (2 * (order % 4) + order // 4)
        for part in range(3):
            start = pl.multiple_of((owner * 3 + part) * rows, rows)
            out_ref[order, part] = sums[pl.ds(start, rows), :].astype(LOW)


def keep_kernel(groups, place_ref, received_ref, *refs):
    give_ref, keep_ref, sums = refs[-3:]
    shard, core, plane = place_ref[0], place_ref[1], place_ref[2]
    products(groups, refs[:-3], core, sums)
    rows = give_ref.shape[1]
    for order in range(8):
        owner = shard ^ (2 * (order % 4) + order // 4)

        def total(part):
            start = pl.multiple_of((owner * 3 + part) * rows, rows)
            mine = sums[pl.ds(start, rows), :]
            return (mine + received_ref[order, part].astype(WIDE)).astype(LOW)

        give_ref[order] = total(1 - plane)
        keep_ref[0, order] = total(plane)
        keep_ref[1, order] = total(2)


class Reduction:
    def __init__(self, place, groups):
        self.place = place
        self.counts = tuple(len(group) - 1 for group in groups)
        self.operands = [entry for group in groups for entry in group]
        self.height = sum(entry.shape[0] for entry in groups[0][:-1])
        self.half = sum(group[-1].shape[1] for group in groups) // 2
        self.rows = self.height // 24
        self.scratch = [pltpu.VMEM((self.height, self.half), WIDE)]
        self.cost = cost(2 * self.height * self.half * ROW, 4 * self.height * self.half)

    def give(self):
        return pl.pallas_call(
            partial(give_kernel, self.counts),
            out_shape=shape((8, 3, self.rows, self.half)),
            in_specs=[in_smem()] + [in_vmem()] * len(self.operands),
            out_specs=in_vmem(),
            scratch_shapes=self.scratch,
            compiler_params=kernel_params(10),
            cost_estimate=self.cost,
        )(self.place, *self.operands)

    def keep(self, received):
        return pl.pallas_call(
            partial(keep_kernel, self.counts),
            out_shape=[shape((8, self.rows, self.half)), shape((2, 8, self.rows, self.half))],
            in_specs=[in_smem()] + [in_vmem()] * (1 + len(self.operands)),
            out_specs=[in_vmem()] * 2,
            scratch_shapes=self.scratch,
            compiler_params=kernel_params(12),
            cost_estimate=self.cost,
        )(self.place, received, *self.operands)

    def after_y(self, kept, side):
        sent = jnp.stack([plus(kept[0, 4:], side[4:]), kept[1, 4:]])
        return sent, (kept[0, :4], side[:4], kept[1, :4])

    def after_x(self, stay, column):
        kept, side, shared = stay
        return [
            jnp.stack([plus(kept[step], side[step], column[0, step]), plus(shared[step], column[1, step])])
            for step in range(4)
        ]

    def over_z(self, columns, name):
        return [swap(columns[step], "shard", 2 * step, name) for step in (1, 2, 3)]

    def after_z(self, mine, pieces):
        piece = plus(mine, *pieces)
        for bit in range(2, lax.axis_size("dp").bit_length() - 1):
            piece = plus(piece, swap(piece, "dp", 2**bit))
        return piece

    def after_y2(self, piece, other):
        shared = plus(piece[1], other[1])
        even = self.place[2] == 0
        first = jnp.where(even, piece[0], other[0])
        second = jnp.where(even, other[0], piece[0])
        return jnp.stack([first, second, shared])

    def halves(self, mine, theirs):
        low_core = self.place[1] == 0
        low, high = jnp.where(low_core, mine, theirs), jnp.where(low_core, theirs, mine)
        return low.reshape(3 * self.rows, self.half), high.reshape(3 * self.rows, self.half)


def plus(*entries):
    return sum(entry.astype(WIDE) for entry in entries).astype(LOW)


def total(entry, axes):
    for axis in axes:
        for bit in range(lax.axis_size(axis).bit_length() - 1):
            entry = entry + swap(entry, axis, 2**bit)
    return entry


def body(
    tokens,
    picture_ids,
    cotangent,
    w_qkv,
    w_out,
    w_fc1,
    w_fc2,
    vectors,
    fc1_bias,
    moments_qkv,
    moments_out,
    moments_fc1,
    moments_fc2,
    moments_vectors,
    moments_fc1_bias,
):
    model_width = tokens.shape[1]
    masters = (w_qkv, w_out, w_fc1, w_fc2, vectors, fc1_bias)
    moments = (
        moments_qkv,
        moments_out,
        moments_fc1,
        moments_fc2,
        moments_vectors,
        moments_fc1_bias,
    )
    shard = lax.axis_index("shard")
    data = lax.axis_index("dp")
    place = jnp.stack([shard, data % 2, (data // 2) % 2]).astype(jnp.int32)
    model_owned = vectors.shape[1]
    hidden_owned = fc1_bias.shape[0]
    valid = (picture_ids != 0).astype(WIDE)[:, None]
    own_a, own_b, own_c = own_pieces(place, w_qkv, w_out, w_fc1, w_fc2, vectors, fc1_bias)
    near_a = jnp.stack(gather_z(own_a, "A"), axis=1)
    near_a, own_b, own_c = sync(near_a, own_b, own_c)
    far_a, near2_a = gather_x(near_a, "A"), gather_core(near_a, "A")
    near_b = jnp.stack(gather_z(own_b, "B"), axis=1)
    far_a, near_b = sync(far_a, near_b)
    side_a = gather_y(near_a, far_a, "A", w_qkv.shape[1] // 2)
    far_b, near2_b = gather_x(near_b, "B"), gather_core(near_b, "B")
    far2_a, side2_a = gather_core(far_a, "A"), gather_core(side_a, "A")
    near_c = jnp.stack(gather_z(own_c, "C"), axis=1)
    pieces_a = (near_a, far_a, side_a, near2_a, far2_a, side2_a)
    far_b, near_c, side2_a = sync(far_b, near_c, side2_a)
    side_b, far2_b = gather_y(near_b, far_b, "B"), gather_core(far_b, "B")
    far_c, near2_c = gather_x(near_c, "C"), gather_core(near_c, "C")
    vec, bias, a1_t, mix, mix_t, qkv, prob = attention(
        place, after(tokens, far_b, near_c), picture_ids, w_fc1.shape[1], pieces_a
    )
    side_b, far2_b, mix = sync(side_b, far2_b, mix)
    side2_b = gather_core(side_b, "B")
    pieces_b = (near_b, far_b, side_b, near2_b, far2_b, side2_b)
    mid, a2_t, act, act_t, slope, sums_in, wide_out, wide_fc1 = hidden_layer(
        place, tokens, mix, valid, vec, bias, pieces_b
    )
    far_c, near2_c, act_t = sync(far_c, near2_c, act_t)
    far2_c = gather_core(far_c, "C")
    fc2 = Reduction(place, [(act_t, cotangent)])
    given = fc2.give()
    far2_c, given = sync(far2_c, given)
    recv_f2 = gather_core(given, "F2")
    pieces_c = (near_c, far_c, near2_c, far2_c)
    d_pre, shift_sum, wide_fc2 = hidden_back(place, cotangent, after(slope, given), pieces_c)
    recv_f2, d_pre = sync(recv_f2, d_pre)
    give_f2, keep_f2 = fc2.keep(recv_f2)
    side_f2 = swap(give_f2, "dp", 2, "F2")
    fc1 = Reduction(place, [(a2_t, after(d_pre, give_f2))])
    given = fc1.give()
    recv_f1 = gather_core(given, "F1")
    layer_out, d_mid, d_mid_low, d_mix, sums_mid = middle_layer(
        mid, act, after(d_pre, given), cotangent, valid, vec, wide_out, wide_fc1, wide_fc2
    )
    recv_f1, d_mix = sync(recv_f1, d_mix)
    give_f1, keep_f1 = fc1.keep(recv_f1)
    side_f2, give_f1, d_mix = sync(side_f2, give_f1, d_mix)
    sent, stay_f2 = fc2.after_y(keep_f2, side_f2)
    column_f2 = swap(sent, "shard", 1, "F2")
    side_f1 = swap(give_f1, "dp", 2, "F1")
    d_proj, sums_att = attention_back(qkv, mix_t, after(d_mix, sent), prob)
    first = Reduction(place, [(a1_t, d_proj), (mix_t, d_mid_low)])
    given = first.give()
    column_f2, side_f1, given = sync(column_f2, side_f1, given)
    recv_a = gather_core(given, "RA")
    columns = fc2.after_x(stay_f2, column_f2)
    pieces_f2, mine_f2 = fc2.over_z(columns, "F2"), columns[0]
    sent, stay_f1 = fc1.after_y(keep_f1, side_f1)
    column_f1 = swap(sent, "shard", 1, "F1")
    tokens_grad, sums_first = first_norm_back(
        place, tokens, d_proj, after(d_mid, columns, sent), vec, pieces_a
    )
    recv_a, sums_first = sync(recv_a, sums_first)
    give_a, keep_a = first.keep(recv_a)
    side_ra = swap(give_a, "dp", 2, "RA")
    small_sums = jnp.concatenate(
        [
            sums_first[:2],
            sums_att[:2],
            sums_mid[:4],
            shift_sum.reshape(-1, model_width),
            sums_in[:3],
            sums_mid[4:6],
            jnp.full((1, model_width), jnp.sum(valid)),
        ]
    )
    small_more = swap(small_sums, "dp", 1)
    pieces_f2, column_f1, give_a, small_more = sync(pieces_f2, column_f1, give_a, small_more)
    small_sums = small_sums + small_more
    columns = fc1.after_x(stay_f1, column_f1)
    pieces_f1, mine_f1 = fc1.over_z(columns, "F1"), columns[0]
    piece_f2 = fc2.after_z(mine_f2, pieces_f2)
    other_f2 = swap(piece_f2, "dp", 2, "F2")
    small_more = swap(small_sums, "dp", 2)
    side_ra, other_f2, small_more = sync(side_ra, other_f2, small_more)
    small_sums = small_sums + small_more
    sent, stay_a = first.after_y(keep_a, side_ra)
    column_a = swap(sent, "shard", 1, "RA")
    owned_f2 = fc2.after_y2(piece_f2, other_f2)
    theirs_f2 = gather_core(owned_f2, "F2")
    small_more = swap(small_sums, "shard", 1)
    pieces_f1, column_a, theirs_f2, small_more = sync(pieces_f1, column_a, theirs_f2, small_more)
    small_sums = small_sums + small_more
    columns = first.after_x(stay_a, column_a)
    pieces_ra, mine_a = first.over_z(columns, "RA"), columns[0]
    piece_f1 = fc1.after_z(mine_f1, pieces_f1)
    other_f1 = swap(piece_f1, "dp", 2, "F1")
    small_more = swap(small_sums, "shard", 2)
    pieces_ra, other_f1, small_more = sync(pieces_ra, other_f1, small_more)
    small_sums = small_sums + small_more
    piece_a = first.after_z(mine_a, pieces_ra)
    other_a = swap(piece_a, "dp", 2, "RA")
    owned_f1 = fc1.after_y2(piece_f1, other_f1)
    theirs_f1 = gather_core(owned_f1, "F1")
    small_more = swap(small_sums, "shard", 4)
    other_a, theirs_f1, small_more = sync(other_a, theirs_f1, small_more)
    small_sums = small_sums + small_more
    owned_a = first.after_y2(piece_a, other_a)
    theirs_a = gather_core(owned_a, "RA")
    for bit in range(2, lax.axis_size("dp").bit_length() - 1):
        small_sums = small_sums + swap(small_sums, "dp", 2**bit)
    fc2_halves, fc1_halves = fc2.halves(owned_f2, theirs_f2), fc1.halves(owned_f1, theirs_f1)
    first_halves = first.halves(owned_a, theirs_a)
    split = w_qkv.shape[1] // 2
    owner_grads = [
        jnp.concatenate([half[:, :split] for half in first_halves], axis=1).astype(WIDE),
        jnp.concatenate([half[:, split:] for half in first_halves], axis=1).astype(WIDE),
        jnp.concatenate(fc1_halves, axis=1).astype(WIDE),
        jnp.concatenate(fc2_halves, axis=1).astype(WIDE),
    ]
    grad_vectors, grad_shift = small_sums[:8], small_sums[8:12].reshape(-1)
    stream_sums = jnp.sum(small_sums[12:17], axis=1)
    square_sum = total(sum(jnp.sum(entry * entry) for entry in owner_grads), ("shard",))
    square_sum = square_sum + jnp.sum(small_sums[:12] * small_sums[:12])
    owner_grads = (
        *owner_grads,
        lax.dynamic_slice_in_dim(grad_vectors, shard * model_owned, model_owned, 1),
        lax.dynamic_slice_in_dim(grad_shift, shard * hidden_owned, hidden_owned, 0),
    )
    stream_rms = jnp.sqrt(stream_sums / (small_sums[17, 0] * model_width))
    clip_factor = CLIP_NORM / jnp.maximum(jnp.sqrt(square_sum), CLIP_NORM)
    correction = 1.0 - ADAM_BETA**STEP
    updated = []
    for number in range(6):
        clipped = owner_grads[number] * clip_factor
        first_moment = ADAM_BETA * moments[number][0] + (1.0 - ADAM_BETA) * clipped
        second_moment = ADAM_BETA * moments[number][1] + (1.0 - ADAM_BETA) * clipped * clipped
        change = first_moment / correction / (jnp.sqrt(second_moment / correction) + ADAM_EPS)
        if number < 4:
            change = change + WEIGHT_DECAY * masters[number]
        if number == 4:
            updated.append(LEARN_RATE * change)
        else:
            updated.append(masters[number] - LEARN_RATE * change)
    return (layer_out, tokens_grad, *owner_grads, *updated, stream_rms)


def solution(mesh):
    placed = (
        P(("dp", "shard"), None),
        P(("dp", "shard")),
        P(("dp", "shard"), None),
        P("shard", None),
        P("shard", None),
        P("shard", None),
        P("shard", None),
        P(None, "shard"),
        P("shard"),
        P(None, "shard", None),
        P(None, "shard", None),
        P(None, "shard", None),
        P(None, "shard", None),
        P(None, None, "shard"),
        P(None, "shard"),
    )
    return jax.shard_map(
        body,
        mesh=mesh,
        in_specs=placed,
        out_specs=(
            P(("dp", "shard"), None),
            P(("dp", "shard"), None),
            P("shard", None),
            P("shard", None),
            P("shard", None),
            P("shard", None),
            P(None, "shard"),
            P("shard"),
            P("shard", None),
            P("shard", None),
            P("shard", None),
            P("shard", None),
            P(None, "shard"),
            P("shard"),
            P(),
        ),
        check_vma=False,
    )
```

time: 899 us -> 315 us (0.35)
  waiting for transfers between devices: 531 us -> 110 us
  blocking collectives: 173 us -> 0 us
  matrix products: 85.7 us -> 0 us
  Pallas kernels: 0 us -> 82.5 us
  starting transfers between devices: 0.5 us -> 64.3 us
  local copies, waits for them, and re-layouts: 36.6 us -> 13.4 us
  between operations: 20.9 us -> 7.87 us
  other arithmetic: 43 us -> 30.4 us
    reduce_scatter x4 -> x0, waiting for transfers between devices: 348 us -> none  [the longest x1 132 us: body(): lax.psum_scatter(ordered[2], ('dp', 'shard'), scatter_dimension=0, tiled=...]
    all_gather x4 -> x0, waiting for transfers between devices: 183 us -> none  [the longest x1 77.5 us: body(): lax.all_gather(w_fc1.astype(jnp.bfloat16), 'shard', axis=0, tiled=True)]
    ppermute x0 -> x54, waiting for transfers between devices: none -> 110 us  [swap(): lax.ppermute(entry, axis, [(place, place ^ mask) for place in range(count)])]
    all_gather x7 -> x0, blocking collectives: 87.2 us -> none  [the longest x1 28 us: body(): lax.all_gather(fc1_bias.astype(jnp.bfloat16), 'shard', axis=0, tiled=True)]
    dot_general x18 -> x0, matrix products: 85.7 us -> none  [the longest x1 13.6 us: attend_backward(): jnp.einsum('qhd,khd->hqk', grad_mix, values_in, preferred_element_type=jn...]
    pallas_call x0 -> x13, Pallas kernels: none -> 82.5 us  [the longest x1 19.6 us: attention(): pl.pallas_call(attention_kernel, out_shape=[shape((8, width), WIDE), shap...]
    ppermute x0 -> x54, starting transfers between devices: none -> 64.3 us  [swap(): lax.ppermute(entry, axis, [(place, place ^ mask) for place in range(count)])]
    unnamed x2 -> x0, blocking collectives: 46.8 us -> none
  transfers between devices with their start and end apart: 8 -> 54, of which waited for: 7 -> 24; matrix products, arithmetic and copies ran while one was open for 13% -> 6% of each run, Pallas kernels for 0% -> 24%
where the time goes in v1:
time: 315 us; the launch traced here: 309 us
  waiting for transfers between devices  110 us (35%)
  Pallas kernels  82.5 us (26%)
  starting transfers between devices  64.3 us (20%)
  other arithmetic  30.4 us (10%)
  local copies, waits for them, and re-layouts  13.4 us (4%)
  between operations  7.87 us (2%)
    ppermute x54, waiting for transfers between devices, swap(): lax.ppermute(entry, axis, [(place, place ^ mask) for place in range(count)])  110 us
    ppermute x54, starting transfers between devices, swap(): lax.ppermute(entry, axis, [(place, place ^ mask) for place in range(count)])  64.3 us
    pallas_call x1, Pallas kernels, attention(): pl.pallas_call(attention_kernel, out_shape=[shape((8, width), WIDE), shap...  19.6 us
    pallas_call x1, Pallas kernels, attention_back(): pl.pallas_call(attention_back_kernel, out_shape=[shape((ROW, 3 * width)),...  12.3 us
    pallas_call x1, Pallas kernels, hidden_layer(): pl.pallas_call(hidden_kernel, out_shape=[shape((ROW, width), WIDE), shape...  10.5 us
    pallas_call x3, Pallas kernels, keep(): pl.pallas_call(partial(keep_kernel, self.counts), out_shape=[shape((8, se...  9.99 us
    sub x5, other arithmetic, body(): updated.append(masters[number] - LEARN_RATE * change)  9.85 us
    pallas_call x3, Pallas kernels, give(): pl.pallas_call(partial(give_kernel, self.counts), out_shape=shape((8, 3,...  9.12 us
  transfers between devices with their start and end apart: 54, of which 24 were waited for; matrix products, arithmetic and copies ran while one was open for 6% of the time, Pallas kernels for 24%

profile of v1, /device:TPU:0, one launch (start us, length us, event | category | flops | bytes accessed | tf_op | source)
XLA Modules:
  0.0 308.5 jit_solution(8384948170030983087)
XLA Ops:
  2.1 2.1 shard_map.262
  4.2 5.1 %collective-permute-start.2 = (bf16[2,32,1280]{2,1,0:T(8,128)(2,1)S(1)}, bf16[2,32,1280]{2,1,0:T(8,128)(2,1)S(1)}, u32[]{:S(2)}, u32[]{:S(2)}) collective-permute-start(bf16[2,32,1280]{2,1,0:T(8,128)(2,1)S(1)} %get-tuple-element.106), channel_id=1, source_target_pairs={{0,6},{1,7},{2,4},{3,5},{4,2},{5,3},{6,0},{7,1},{8,14},{9,15},{10,... | collective-permute-start | bytes 491528 | tf_op jit(solution)/shard_map/A_shard6/ppermute | solution.py:32
  10.0 4.5 %collective-permute-done.2 = bf16[2,32,1280]{2,1,0:T(8,128)(2,1)S(1)} collective-permute-done((bf16[2,32,1280]{2,1,0:T(8,128)(2,1)S(1)}, bf16[2,32,1280]{2,1,0:T(8,128)(2,1)S(1)}, u32[]{:S(2)}, u32[]{:S(2)}) %collective-permute-start.2) | collective-permute-done | bytes 163872 | tf_op jit(solution)/shard_map/A_shard6/ppermute | solution.py:32
  14.5 8.8 %collective-permute-done.1 = bf16[2,32,1280]{2,1,0:T(8,128)(2,1)S(1)} collective-permute-done((bf16[2,32,1280]{2,1,0:T(8,128)(2,1)S(1)}, bf16[2,32,1280]{2,1,0:T(8,128)(2,1)S(1)}, u32[]{:S(2)}, u32[]{:S(2)}) %collective-permute-start.1) | collective-permute-done | bytes 163872 | tf_op jit(solution)/shard_map/A_shard4/ppermute | solution.py:32
  23.3 2.6 collective-permute-start.6
  25.9 1.9 collective-permute-start.4
  27.8 1.5 collective-permute-start.3
  29.3 4.9 %collective-permute-done.6 = bf16[2,32,1920]{2,1,0:T(8,128)(2,1)S(1)} collective-permute-done((bf16[2,32,1920]{2,1,0:T(8,128)(2,1)S(1)}, bf16[2,32,1920]{2,1,0:T(8,128)(2,1)S(1)}, u32[]{:S(2)}, u32[]{:S(2)}) %collective-permute-start.6) | collective-permute-done | bytes 245792 | tf_op jit(solution)/shard_map/B_shard6/ppermute | solution.py:32
  34.2 10.9 %collective-permute-done.5 = bf16[2,32,1920]{2,1,0:T(8,128)(2,1)S(1)} collective-permute-done((bf16[2,32,1920]{2,1,0:T(8,128)(2,1)S(1)}, bf16[2,32,1920]{2,1,0:T(8,128)(2,1)S(1)}, u32[]{:S(2)}, u32[]{:S(2)}) %collective-permute-start.5) | collective-permute-done | bytes 245792 | tf_op jit(solution)/shard_map/B_shard4/ppermute | solution.py:32
  46.3 1.6 collective-permute-start.11
  47.9 1.5 collective-permute-start.7
  49.4 1.7 collective-permute-start.10
  51.1 2.7 collective-permute-start.8
  53.8 5.9 %collective-permute-done.11.refs_2_ = bf16[8,32,1152]{2,1,0:T(8,128)(2,1)S(1)} collective-permute-done((bf16[8,32,1152]{2,1,0:T(8,128)(2,1)S(1)}, bf16[8,32,1152]{2,1,0:T(8,128)(2,1)S(1)}, u32[]{:S(2)}, u32[]{:S(2)}) %collective-permute-start.11) | collective-permute-done | bytes 589856 | tf_op jit(solution)/shard_map/A_dp2/ppermute | solution.py:32
  59.7 1.5 collective-permute-done.10
  61.1 12.4 %collective-permute-done.9 = bf16[3,128,384]{2,1,0:T(8,128)(2,1)S(1)} collective-permute-done((bf16[3,128,384]{2,1,0:T(8,128)(2,1)S(1)}, bf16[3,128,384]{2,1,0:T(8,128)(2,1)S(1)}, u32[]{:S(2)}, u32[]{:S(2)}) %collective-permute-start.9) | collective-permute-done | bytes 294944 | tf_op jit(solution)/shard_map/C_shard4/ppermute | solution.py:32
  75.8 1.3 slice_bitcast_fusion
  79.7 3.0 collective-permute-done.15.refs_3_
  85.3 19.6 %shard_map.263 = (f32[8,768]{1,0:T(8,128)S(1)}, f32[1,3072]{1,0:T(1,128)S(1)}, bf16[768,512]{1,0:T(8,128)(2,1)S(1)}, bf16[512,768]{1,0:T(8,128)(2,1)S(1)}, bf16[...) custom-call(s32[3]{0:T(128)S(1)} %pad_add_fusion.place_ref, ...), custom_call_target="tpu_custom_call" | custom-call | flops 1 | bytes 1 | tf_op jit(solution)/shard_map/pallas_call | solution.py:270
  106.3 2.4 collective-permute-done.18.refs_5_
  108.7 10.5 %shard_map.264 = (f32[512,768]{1,0:T(8,128)S(1)}, bf16[768,512]{1,0:T(8,128)(2,1)S(1)}, bf16[512,3072]{1,0:T(8,128)(2,1)S(1)}, bf16[3072,512]{1,0:T(8,128)(2,1)S...) custom-call(s32[3]{0:T(128)S(1)} %pad_add_fusion.place_ref, ...), custom_call_target="tpu_custom_call" | custom-call | flops 1 | bytes 1 | tf_op jit(solution)/shard_map/pallas_call | solution.py:337
  119.7 2.6 shard_map.265
  123.4 5.7 %shard_map.266 = (bf16[512,3072]{1,0:T(8,128)(2,1)S(1)}, f32[1,3072]{1,0:T(1,128)S(1)}, bf16[3072,768]{1,0:T(8,128)(2,1)S(1)}) custom-call(s32[3]{0:T(128)S(1)} %pad_add_fusion.place_ref, bf16[512,768]{1,0:T(8,128)(2,1)S(1)} %copy-done, bf16[512,3072]{1,0:T(8,128)(2,1)S(1)} %get-tuple-element.130.slope_ref, ...), custom_call_target="tpu_custom_call" | custom-call | flops 1 | bytes 1 | tf_op jit(solution)/shard_map/pallas_call | solution.py:377
  129.0 3.1 shard_map.267
  132.1 2.6 shard_map.268
  135.1 1.5 collective-permute-start.23
  136.7 7.1 %shard_map.269 = (bf16[512,768]{1,0:T(8,128)(2,1)}, f32[512,768]{1,0:T(8,128)S(1)}, bf16[512,768]{1,0:T(8,128)(2,1)S(1)}, bf16[512,768]{1,0:T(8,128)(2,1)S(1)}, f32[8,768]{1,0:T(8,128)S(1)}) custom-call(f32[512,768]{1,0:T(8,128)S(1)} %get-tuple-element.123.mid_ref, bf16[512,3072]{1,0:T(8,128)(2,1)S(1)} %get-tuple-element.124.act_ref, ...), custom_call_target="tpu_custom_call" | custom-call | flops 1 | bytes 1 | tf_op jit(solution)/shard_map/pallas_call | solution.py:415
  143.9 2.8 shard_map.270
  146.7 8.0 %collective-permute-done.23 = bf16[8,128,384]{2,1,0:T(8,128)(2,1)S(1)} collective-permute-done((bf16[8,128,384]{2,1,0:T(8,128)(2,1)S(1)}, bf16[8,128,384]{2,1,0:T(8,128)(2,1)S(1)}, u32[]{:S(2)}, u32[]{:S(2)}) %collective-permute-start.23) | collective-permute-done | bytes 786464 | tf_op jit(solution)/shard_map/F2_dp2/ppermute | solution.py:32
  156.1 1.5 collective-permute-start.26
  157.7 12.3 %shard_map.271 = (bf16[512,2304]{1,0:T(8,128)(2,1)S(1)}, f32[8,768]{1,0:T(8,128)S(1)}) custom-call(bf16[512,2304]{1,0:T(8,128)(2,1)S(1)} %copy-done.8, bf16[768,512]{1,0:T(8,128)(2,1)S(1)} %get-tuple-element.145.mix_t_ref.refs_2_, bf16[512,768]{1,0:T(8,128)(2,1)S(1)} %get-tuple-element.153.d_mix_ref, bf16[12,512,512]{2,1,0:T(8,128)(2,1)} %get-tuple-element.154.prob_in), custom_call_target="tpu_custom_call" | custom-call | flops 1 | bytes 1 | tf_op jit(solution)/shard_map/pallas_call | solution.py:487
  170.0 4.0 %shard_map.272 = bf16[8,3,32,1536]{3,2,1,0:T(8,128)(2,1)} custom-call(s32[3]{0:T(128)S(1)} %pad_add_fusion.place_ref, bf16[768,512]{1,0:T(8,128)(2,1)S(1)} %copy-done.4, bf16[512,2304]{1,0:T(8,128)(2,1)S(1)} %get-tuple-element.155.refs_1_.d_proj_ref, bf16[768,512]{1,0:T(8,128)(2,1)S(1)} %get-tuple-element.145.mix_t_ref.refs_2_, ...), custom_call_target="tpu_custom_call" | custom-call | flops 1 | bytes 1 | tf_op jit(solution)/shard_map/pallas_call | solution.py:594
  177.9 1.4 fusion.31
  180.2 1.5 collective-permute-start.32
  183.4 2.6 collective-permute-start.30
  186.7 1.8 collective-permute-start.31
  188.5 6.1 %shard_map.273 = (bf16[512,768]{1,0:T(8,128)(2,1)}, f32[8,768]{1,0:T(8,128)S(1)}) custom-call(s32[3]{0:T(128)S(1)} %pad_add_fusion.place_ref, bf16[512,768]{1,0:T(8,128)(2,1)S(1)} %copy-done.2, bf16[512,2304]{1,0:T(8,128)(2,1)S(1)} %get-tuple-element.155.refs_1_.d_proj_ref, f32[512,768]{1,0:T(8,128)S(1)} %copy-done.18, ...), custom_call_target="tpu_custom_call" | custom-call | flops 4000000000 | bytes 1 | tf_op jit(solution)/shard_map/pallas_call | solution.py:520
  198.1 4.1 %shard_map.274 = (bf16[8,32,1536]{2,1,0:T(8,128)(2,1)S(1)}, bf16[2,8,32,1536]{3,2,1,0:T(8,128)(2,1)S(1)}) custom-call(s32[3]{0:T(128)S(1)} %pad_add_fusion.place_ref, bf16[8,3,32,1536]{3,2,1,0:T(8,128)(2,1)} %collective-permute-done.27.received_ref, bf16[768,512]{1,0:T(8,128)(2,1)S(1)} %copy-done.5, ...), custom_call_target="tpu_custom_call" | custom-call | flops 1 | bytes 1 | tf_op jit(solution)/shard_map/pallas_call | solution.py:605
  202.2 1.6 collective-permute-start.28
  206.8 1.9 collective-permute-start.36
  208.7 1.2 add_convert_fusion.2
  210.5 1.9 collective-permute-start.37
  212.3 11.8 %collective-permute-done.35 = f32[18,768]{1,0:T(8,128)S(1)} collective-permute-done((f32[18,768]{1,0:T(8,128)S(1)}, f32[18,768]{1,0:T(8,128)S(1)}, u32[]{:S(2)}, u32[]{:S(2)}) %collective-permute-start.35) | collective-permute-done | bytes 55328 | tf_op jit(solution)/shard_map/sums_dp2/ppermute | solution.py:32
  224.2 3.8 %collective-permute-done.34 = bf16[2,128,384]{2,1,0:T(8,128)(2,1)S(1)} collective-permute-done((bf16[2,128,384]{2,1,0:T(8,128)(2,1)S(1)}, bf16[2,128,384]{2,1,0:T(8,128)(2,1)S(1)}, u32[]{:S(2)}, u32[]{:S(2)}) %collective-permute-start.34) | collective-permute-done | bytes 196640 | tf_op jit(solution)/shard_map/F2_dp2/ppermute | solution.py:32
  229.0 2.1 collective-permute-start.38
  231.1 1.6 collective-permute-start.41
  232.7 5.6 %collective-permute-done.38 = bf16[2,32,1536]{2,1,0:T(8,128)(2,1)S(1)} collective-permute-done((bf16[2,32,1536]{2,1,0:T(8,128)(2,1)S(1)}, bf16[2,32,1536]{2,1,0:T(8,128)(2,1)S(1)}, u32[]{:S(2)}, u32[]{:S(2)}) %collective-permute-start.38) | collective-permute-done | bytes 196640 | tf_op jit(solution)/shard_map/F1_shard6/ppermute | solution.py:32
  238.3 10.7 %collective-permute-done.41 = f32[18,768]{1,0:T(8,128)S(1)} collective-permute-done((f32[18,768]{1,0:T(8,128)S(1)}, f32[18,768]{1,0:T(8,128)S(1)}, u32[]{:S(2)}, u32[]{:S(2)}) %collective-permute-start.41) | collective-permute-done | bytes 55328 | tf_op jit(solution)/shard_map/sums_shard1/ppermute | solution.py:32
  249.4 2.7 collective-permute-start.43
  252.1 1.8 collective-permute-start.44
  254.0 1.6 collective-permute-start.45
  256.3 6.5 %collective-permute-done.46 = f32[18,768]{1,0:T(8,128)S(1)} collective-permute-done((f32[18,768]{1,0:T(8,128)S(1)}, f32[18,768]{1,0:T(8,128)S(1)}, u32[]{:S(2)}, u32[]{:S(2)}) %collective-permute-start.46) | collective-permute-done | bytes 55328 | tf_op jit(solution)/shard_map/sums_shard2/ppermute | solution.py:32
  262.8 3.5 %collective-permute-done.43 = bf16[2,32,1536]{2,1,0:T(8,128)(2,1)S(1)} collective-permute-done((bf16[2,32,1536]{2,1,0:T(8,128)(2,1)S(1)}, bf16[2,32,1536]{2,1,0:T(8,128)(2,1)S(1)}, u32[]{:S(2)}, u32[]{:S(2)}) %collective-permute-start.43) | collective-permute-done | bytes 196640 | tf_op jit(solution)/shard_map/RA_shard4/ppermute | solution.py:32
  266.5 1.6 collective-permute-start.47
  268.3 3.5 %collective-permute-start.49 = (f32[18,768]{1,0:T(8,128)S(1)}, f32[18,768]{1,0:T(8,128)S(1)}, u32[]{:S(2)}, u32[]{:S(2)}) collective-permute-start(f32[18,768]{1,0:T(8,128)S(1)} %add.465), channel_id=1, source_target_pairs={{0,4},{1,5},{2,6},{3,7},{4,0},{5,1},{6,2},{7,3},{8,12},{9,13},{10,... | collective-permute-start | bytes 165896 | tf_op jit(solution)/shard_map/sums_shard4/ppermute | solution.py:32
  272.8 2.0 collective-permute-done.49
  282.8 1.9 collective-permute-start.51
  284.7 1.7 collective-permute-done.51
  287.1 3.5 %collective-permute-start.52 = (f32[]{:T(128)}, f32[]{:T(128)}, u32[]{:S(2)}, u32[]{:S(2)}) collective-permute-start(f32[]{:T(128)} %add.473), channel_id=1, source_target_pairs={{0,2},{1,3},{2,0},{3,1},{4,6},{5,7},{6,4},{7,5},{8,10},{9,11},{10,... | collective-permute-start | bytes 20 | tf_op jit(solution)/shard_map/sums_shard2/ppermute | solution.py:32
  291.4 3.9 %collective-permute-start.53 = (f32[]{:T(128)}, f32[]{:T(128)}, u32[]{:S(2)}, u32[]{:S(2)}) collective-permute-start(f32[]{:T(128)} %add.474), channel_id=1, source_target_pairs={{0,4},{1,5},{2,6},{3,7},{4,0},{5,1},{6,2},{7,3},{8,12},{9,13},{10,... | collective-permute-start | bytes 20 | tf_op jit(solution)/shard_map/sums_shard4/ppermute | solution.py:32
  297.3 2.2 fusion.37
  299.5 3.2 %fusion.22 = f32[96,2304]{1,0:T(8,128)} fusion(f32[96,2304]{1,0:T(8,128)S(1)} %copy-done.25, f32[2,96,2304]{2,1,0:T(8,128)} %param.24, f32[96,2304]{1,0:T(8,128)S(1)} %get-tuple-element.210, f32[]{:T(128)S(6)} %div.74), kind=kLoop, calls=%fused_computation.33 | loop fusion | flops 3317760 | bytes 4423684 | tf_op jit(solution)/shard_map/sub | solution.py:831
  302.7 1.9 fusion.13
  305.0 1.9 fusion.4
  (238 shorter events, 40.4 us)
Async XLA Ops:
  4.2 10.2 %collective-permute-start.2 = (bf16[2,32,1280]{2,1,0:T(8,128)(2,1)S(1)}, bf16[2,32,1280]{2,1,0:T(8,128)(2,1)S(1)}, u32[]{:S(2)}, u32[]{:S(2)}) collective-permute-start(bf16[2,32,1280]{2,1,0:T(8,128)(2,1)S(1)} %get-tuple-element.106), channel_id=1, source_target_pairs={{0,6},{1,7},{2,4},{3,5},{4,2},{5,3},{6,0},{7,1},{8,14},{9,15},{10,... | collective-permute-start | bytes 491528 | tf_op jit(solution)/shard_map/A_shard6/ppermute | solution.py:32
  9.3 13.9 %collective-permute-start.1 = (bf16[2,32,1280]{2,1,0:T(8,128)(2,1)S(1)}, bf16[2,32,1280]{2,1,0:T(8,128)(2,1)S(1)}, u32[]{:S(2)}, u32[]{:S(2)}) collective-permute-start(bf16[2,32,1280]{2,1,0:T(8,128)(2,1)S(1)} %get-tuple-element.106), channel_id=1, source_target_pairs={{0,4},{1,5},{2,6},{3,7},{4,0},{5,1},{6,2},{7,3},{8,12},{9,13},{10,... | collective-permute-start | bytes 491528 | tf_op jit(solution)/shard_map/A_shard4/ppermute | solution.py:32
  9.3 13.9 %collective-permute-start = (bf16[2,32,1280]{2,1,0:T(8,128)(2,1)S(1)}, bf16[2,32,1280]{2,1,0:T(8,128)(2,1)S(1)}, u32[]{:S(2)}, u32[]{:S(2)}) collective-permute-start(bf16[2,32,1280]{2,1,0:T(8,128)(2,1)S(1)} %get-tuple-element.106), channel_id=1, source_target_pairs={{0,2},{1,3},{2,0},{3,1},{4,6},{5,7},{6,4},{7,5},{8,10},{9,11},{10,... | collective-permute-start | bytes 491528 | tf_op jit(solution)/shard_map/A_shard2/ppermute | solution.py:32
  23.3 55.4 %copy-start.23 = (bf16[2,4,32,1280]{3,2,1,0:T(8,128)(2,1)}, bf16[2,4,32,1280]{3,2,1,0:T(8,128)(2,1)S(1)}, u32[]{:S(2)}) copy-start(bf16[2,4,32,1280]{3,2,1,0:T(8,128)(2,1)S(1)} %pad_maximum_fusion.6.refs_0_) | copy-start | bytes 1966084
  23.3 10.9 %collective-permute-start.6 = (bf16[2,32,1920]{2,1,0:T(8,128)(2,1)S(1)}, bf16[2,32,1920]{2,1,0:T(8,128)(2,1)S(1)}, u32[]{:S(2)}, u32[]{:S(2)}) collective-permute-start(bf16[2,32,1920]{2,1,0:T(8,128)(2,1)S(1)} %get-tuple-element.110), channel_id=1, source_target_pairs={{0,6},{1,7},{2,4},{3,5},{4,2},{5,3},{6,0},{7,1},{8,14},{9,15},{10,... | collective-permute-start | bytes 737288 | tf_op jit(solution)/shard_map/B_shard6/ppermute | solution.py:32
  25.9 19.2 %collective-permute-start.5 = (bf16[2,32,1920]{2,1,0:T(8,128)(2,1)S(1)}, bf16[2,32,1920]{2,1,0:T(8,128)(2,1)S(1)}, u32[]{:S(2)}, u32[]{:S(2)}) collective-permute-start(bf16[2,32,1920]{2,1,0:T(8,128)(2,1)S(1)} %get-tuple-element.110), channel_id=1, source_target_pairs={{0,4},{1,5},{2,6},{3,7},{4,0},{5,1},{6,2},{7,3},{8,12},{9,13},{10,... | collective-permute-start | bytes 737288 | tf_op jit(solution)/shard_map/B_shard4/ppermute | solution.py:32
  25.9 19.2 %collective-permute-start.4 = (bf16[2,32,1920]{2,1,0:T(8,128)(2,1)S(1)}, bf16[2,32,1920]{2,1,0:T(8,128)(2,1)S(1)}, u32[]{:S(2)}, u32[]{:S(2)}) collective-permute-start(bf16[2,32,1920]{2,1,0:T(8,128)(2,1)S(1)} %get-tuple-element.110), channel_id=1, source_target_pairs={{0,2},{1,3},{2,0},{3,1},{4,6},{5,7},{6,4},{7,5},{8,10},{9,11},{10,... | collective-permute-start | bytes 737288 | tf_op jit(solution)/shard_map/B_shard2/ppermute | solution.py:32
  27.8 18.4 %collective-permute-start.3 = (bf16[2,4,32,1280]{3,2,1,0:T(8,128)(2,1)S(1)}, bf16[2,4,32,1280]{3,2,1,0:T(8,128)(2,1)S(1)}, u32[]{:S(2)}, u32[]{:S(2)}) collective-permute-start(bf16[2,4,32,1280]{3,2,1,0:T(8,128)(2,1)S(1)} %pad_maximum_fusion.6.refs_0_), channel_id=1, source_target_pairs={{0,1},{1,0},{2,3},{3,2},{4,5},{5,4},{6,7},{7,6},{8,9},{9,8},{10,11... | collective-permute-start | bytes 1966088 | tf_op jit(solution)/shard_map/A_shard1/ppermute | solution.py:32
  46.2 33.0 %copy-start.28 = (bf16[2,4,32,1280]{3,2,1,0:T(8,128)(2,1)}, bf16[2,4,32,1280]{3,2,1,0:T(8,128)(2,1)S(1)}, u32[]{:S(2)}) copy-start(bf16[2,4,32,1280]{3,2,1,0:T(8,128)(2,1)S(1)} %collective-permute-done.3.refs_1_) | copy-start | bytes 1966084
  46.3 13.3 %collective-permute-start.11 = (bf16[8,32,1152]{2,1,0:T(8,128)(2,1)S(1)}, bf16[8,32,1152]{2,1,0:T(8,128)(2,1)S(1)}, u32[]{:S(2)}, u32[]{:S(2)}) collective-permute-start(bf16[8,32,1152]{2,1,0:T(8,128)(2,1)S(1)} %pad_maximum_fusion.7), channel_id=1, source_target_pairs={{0,16},{8,24},{16,0},{24,8},{1,17},{9,25},{17,1},{25,9},{2,18},{10... | collective-permute-start | bytes 1769480 | tf_op jit(solution)/shard_map/A_dp2/ppermute | solution.py:32
  47.9 27.9 %collective-permute-start.7 = (bf16[2,4,32,1920]{3,2,1,0:T(8,128)(2,1)}, bf16[2,4,32,1920]{3,2,1,0:T(8,128)(2,1)}, u32[]{:S(2)}, u32[]{:S(2)}) collective-permute-start(bf16[2,4,32,1920]{3,2,1,0:T(8,128)(2,1)} %pad_maximum_fusion.1.refs_0_), channel_id=1, source_target_pairs={{0,1},{1,0},{2,3},{3,2},{4,5},{5,4},{6,7},{7,6},{8,9},{9,8},{10,11... | collective-permute-start | bytes 2949128 | tf_op jit(solution)/shard_map/B_shard1/ppermute | solution.py:32
  49.4 11.7 %collective-permute-start.10 = (bf16[3,128,384]{2,1,0:T(8,128)(2,1)S(1)}, bf16[3,128,384]{2,1,0:T(8,128)(2,1)S(1)}, u32[]{:S(2)}, u32[]{:S(2)}) collective-permute-start(bf16[3,128,384]{2,1,0:T(8,128)(2,1)S(1)} %get-tuple-element.112), channel_id=1, source_target_pairs={{0,6},{1,7},{2,4},{3,5},{4,2},{5,3},{6,0},{7,1},{8,14},{9,15},{10,... | collective-permute-start | bytes 884744 | tf_op jit(solution)/shard_map/C_shard6/ppermute | solution.py:32
  51.0 22.5 %collective-permute-start.9 = (bf16[3,128,384]{2,1,0:T(8,128)(2,1)S(1)}, bf16[3,128,384]{2,1,0:T(8,128)(2,1)S(1)}, u32[]{:S(2)}, u32[]{:S(2)}) collective-permute-start(bf16[3,128,384]{2,1,0:T(8,128)(2,1)S(1)} %get-tuple-element.112), channel_id=1, source_target_pairs={{0,4},{1,5},{2,6},{3,7},{4,0},{5,1},{6,2},{7,3},{8,12},{9,13},{10,... | collective-permute-start | bytes 884744 | tf_op jit(solution)/shard_map/C_shard4/ppermute | solution.py:32
  51.1 22.5 %collective-permute-start.8 = (bf16[3,128,384]{2,1,0:T(8,128)(2,1)S(1)}, bf16[3,128,384]{2,1,0:T(8,128)(2,1)S(1)}, u32[]{:S(2)}, u32[]{:S(2)}) collective-permute-start(bf16[3,128,384]{2,1,0:T(8,128)(2,1)S(1)} %get-tuple-element.112), channel_id=1, source_target_pairs={{0,2},{1,3},{2,0},{3,1},{4,6},{5,7},{6,4},{7,5},{8,10},{9,11},{10,... | collective-permute-start | bytes 884744 | tf_op jit(solution)/shard_map/C_shard2/ppermute | solution.py:32
  59.7 15.1 %copy-start.39 = (bf16[8,32,1152]{2,1,0:T(8,128)(2,1)}, bf16[8,32,1152]{2,1,0:T(8,128)(2,1)S(1)}, u32[]{:S(2)}) copy-start(bf16[8,32,1152]{2,1,0:T(8,128)(2,1)S(1)} %collective-permute-done.11.refs_2_) | copy-start | bytes 1769476
  59.7 16.1 %collective-permute-start.12 = (bf16[8,32,1152]{2,1,0:T(8,128)(2,1)S(1)}, bf16[8,32,1152]{2,1,0:T(8,128)(2,1)S(1)}, u32[]{:S(2)}, u32[]{:S(2)}) collective-permute-start(bf16[8,32,1152]{2,1,0:T(8,128)(2,1)S(1)} %collective-permute-done.11.refs_2_), channel_id=1, source_target_pairs={{0,8},{8,0},{16,24},{24,16},{1,9},{9,1},{17,25},{25,17},{2,10},{10... | collective-permute-start | bytes 1769480 | tf_op jit(solution)/shard_map/A_dp1/ppermute | solution.py:32
  78.2 27.6 %collective-permute-start.13 = (bf16[8,32,1920]{2,1,0:T(8,128)(2,1)}, bf16[8,32,1920]{2,1,0:T(8,128)(2,1)}, u32[]{:S(2)}, u32[]{:S(2)}) collective-permute-start(bf16[8,32,1920]{2,1,0:T(8,128)(2,1)} %pad_maximum_fusion.2), channel_id=1, source_target_pairs={{0,16},{8,24},{16,0},{24,8},{1,17},{9,25},{17,1},{25,9},{2,18},{10... | collective-permute-start | bytes 2949128 | tf_op jit(solution)/shard_map/B_dp2/ppermute | solution.py:32
  78.7 27.1 %collective-permute-start.14 = (bf16[2,4,32,1920]{3,2,1,0:T(8,128)(2,1)}, bf16[2,4,32,1920]{3,2,1,0:T(8,128)(2,1)}, u32[]{:S(2)}, u32[]{:S(2)}) collective-permute-start(bf16[2,4,32,1920]{3,2,1,0:T(8,128)(2,1)} %collective-permute-done.7.refs_1_), channel_id=1, source_target_pairs={{0,8},{8,0},{16,24},{24,16},{1,9},{9,1},{17,25},{25,17},{2,10},{10... | collective-permute-start | bytes 2949128 | tf_op jit(solution)/shard_map/B_dp1/ppermute | solution.py:32
  78.7 4.1 %collective-permute-start.15 = (bf16[2,4,32,1280]{3,2,1,0:T(8,128)(2,1)S(1)}, bf16[2,4,32,1280]{3,2,1,0:T(8,128)(2,1)S(1)}, u32[]{:S(2)}, u32[]{:S(2)}) collective-permute-start(bf16[2,4,32,1280]{3,2,1,0:T(8,128)(2,1)S(1)} %pad_maximum_fusion.6.refs_0_), channel_id=1, source_target_pairs={{0,8},{8,0},{16,24},{24,16},{1,9},{9,1},{17,25},{25,17},{2,10},{10... | collective-permute-start | bytes 1966088 | tf_op jit(solution)/shard_map/A_dp1/ppermute | solution.py:32
  79.2 5.2 %collective-permute-start.16 = (bf16[2,4,32,1280]{3,2,1,0:T(8,128)(2,1)S(1)}, bf16[2,4,32,1280]{3,2,1,0:T(8,128)(2,1)S(1)}, u32[]{:S(2)}, u32[]{:S(2)}) collective-permute-start(bf16[2,4,32,1280]{3,2,1,0:T(8,128)(2,1)S(1)} %collective-permute-done.3.refs_1_), channel_id=1, source_target_pairs={{0,8},{8,0},{16,24},{24,16},{1,9},{9,1},{17,25},{25,17},{2,10},{10... | collective-permute-start | bytes 1966088 | tf_op jit(solution)/shard_map/A_dp1/ppermute | solution.py:32
  79.3 39.9 %collective-permute-start.20 = (bf16[3,4,128,384]{3,2,1,0:T(8,128)(2,1)}, bf16[3,4,128,384]{3,2,1,0:T(8,128)(2,1)}, u32[]{:S(2)}, u32[]{:S(2)}) collective-permute-start(bf16[3,4,128,384]{3,2,1,0:T(8,128)(2,1)} %pad_maximum_fusion.refs_0_), channel_id=1, source_target_pairs={{0,8},{8,0},{16,24},{24,16},{1,9},{9,1},{17,25},{25,17},{2,10},{10... | collective-permute-start | bytes 3538952 | tf_op jit(solution)/shard_map/C_dp1/ppermute | solution.py:32
  82.8 36.5 %collective-permute-start.19 = (bf16[3,4,128,384]{3,2,1,0:T(8,128)(2,1)}, bf16[3,4,128,384]{3,2,1,0:T(8,128)(2,1)}, u32[]{:S(2)}, u32[]{:S(2)}) collective-permute-start(bf16[3,4,128,384]{3,2,1,0:T(8,128)(2,1)} %pad_maximum_fusion.refs_0_), channel_id=1, source_target_pairs={{0,1},{1,0},{2,3},{3,2},{4,5},{5,4},{6,7},{7,6},{8,9},{9,8},{10,11... | collective-permute-start | bytes 3538952 | tf_op jit(solution)/shard_map/C_shard1/ppermute | solution.py:32
  84.4 21.9 %collective-permute-start.17 = (bf16[2,4,32,1920]{3,2,1,0:T(8,128)(2,1)}, bf16[2,4,32,1920]{3,2,1,0:T(8,128)(2,1)}, u32[]{:S(2)}, u32[]{:S(2)}) collective-permute-start(bf16[2,4,32,1920]{3,2,1,0:T(8,128)(2,1)} %pad_maximum_fusion.1.refs_0_), channel_id=1, source_target_pairs={{0,8},{8,0},{16,24},{24,16},{1,9},{9,1},{17,25},{25,17},{2,10},{10... | collective-permute-start | bytes 2949128 | tf_op jit(solution)/shard_map/B_dp1/ppermute | solution.py:32
  105.8 2.9 collective-permute-start.18
  119.2 3.1 %collective-permute-start.21 = (bf16[3,4,128,384]{3,2,1,0:T(8,128)(2,1)}, bf16[3,4,128,384]{3,2,1,0:T(8,128)(2,1)S(1)}, u32[]{:S(2)}, u32[]{:S(2)}) collective-permute-start(bf16[3,4,128,384]{3,2,1,0:T(8,128)(2,1)} %collective-permute-done.19.refs_1_), channel_id=1, source_target_pairs={{0,8},{8,0},{16,24},{24,16},{1,9},{9,1},{17,25},{25,17},{2,10},{10... | collective-permute-start | bytes 3538952 | tf_op jit(solution)/shard_map/C_dp1/ppermute | solution.py:32
  122.4 6.7 %collective-permute-start.22 = (bf16[8,3,128,384]{3,2,1,0:T(8,128)(2,1)S(1)}, bf16[8,3,128,384]{3,2,1,0:T(8,128)(2,1)S(1)}, u32[]{:S(2)}, u32[]{:S(2)}) collective-permute-start(bf16[8,3,128,384]{3,2,1,0:T(8,128)(2,1)S(1)} %shard_map.265), channel_id=1, source_target_pairs={{0,8},{8,0},{16,24},{24,16},{1,9},{9,1},{17,25},{25,17},{2,10},{10... | collective-permute-start | bytes 7077896 | tf_op jit(solution)/shard_map/F2_dp1/ppermute | solution.py:32
  132.1 22.6 %copy-start.11 = (bf16[2,8,128,384]{3,2,1,0:T(8,128)(2,1)}, bf16[2,8,128,384]{3,2,1,0:T(8,128)(2,1)S(1)}, u32[]{:S(2)}) copy-start(bf16[2,8,128,384]{3,2,1,0:T(8,128)(2,1)S(1)} %get-tuple-element.151) | copy-start | bytes 4718596
  134.7 9.1 %collective-permute-start.24 = (bf16[8,3,32,1536]{3,2,1,0:T(8,128)(2,1)S(1)}, bf16[8,3,32,1536]{3,2,1,0:T(8,128)(2,1)S(1)}, u32[]{:S(2)}, u32[]{:S(2)}) collective-permute-start(bf16[8,3,32,1536]{3,2,1,0:T(8,128)(2,1)S(1)} %shard_map.268), channel_id=1, source_target_pairs={{0,8},{8,0},{16,24},{24,16},{1,9},{9,1},{17,25},{25,17},{2,10},{10... | collective-permute-start | bytes 7077896 | tf_op jit(solution)/shard_map/F1_dp1/ppermute | solution.py:32
  135.1 19.6 %collective-permute-start.23 = (bf16[8,128,384]{2,1,0:T(8,128)(2,1)S(1)}, bf16[8,128,384]{2,1,0:T(8,128)(2,1)S(1)}, u32[]{:S(2)}, u32[]{:S(2)}) collective-permute-start(bf16[8,128,384]{2,1,0:T(8,128)(2,1)S(1)} %get-tuple-element.137), channel_id=1, source_target_pairs={{0,16},{8,24},{16,0},{24,8},{1,17},{9,25},{17,1},{25,9},{2,18},{10... | collective-permute-start | bytes 2359304 | tf_op jit(solution)/shard_map/F2_dp2/ppermute | solution.py:32
  143.8 26.2 %copy-start.6 = (bf16[512,768]{1,0:T(8,128)(2,1)}, bf16[512,768]{1,0:T(8,128)(2,1)S(1)}, u32[]{:S(2)}) copy-start(bf16[512,768]{1,0:T(8,128)(2,1)S(1)} %get-tuple-element.159.refs_3_) | copy-start | bytes 2359300
  155.6 18.8 %collective-permute-start.25 = (bf16[2,4,128,384]{3,2,1,0:T(8,128)(2,1)S(1)}, bf16[2,4,128,384]{3,2,1,0:T(8,128)(2,1)S(1)}, u32[]{:S(2)}, u32[]{:S(2)}) collective-permute-start(bf16[2,4,128,384]{3,2,1,0:T(8,128)(2,1)S(1)} %pad_maximum_fusion.3), channel_id=1, source_target_pairs={{0,1},{1,0},{2,3},{3,2},{4,5},{5,4},{6,7},{7,6},{8,9},{9,8},{10,11... | collective-permute-start | bytes 2359304 | tf_op jit(solution)/shard_map/F2_shard1/ppermute | solution.py:32
  156.1 18.5 %collective-permute-start.26 = (bf16[8,32,1536]{2,1,0:T(8,128)(2,1)S(1)}, bf16[8,32,1536]{2,1,0:T(8,128)(2,1)S(1)}, u32[]{:S(2)}, u32[]{:S(2)}) collective-permute-start(bf16[8,32,1536]{2,1,0:T(8,128)(2,1)S(1)} %get-tuple-element.157), channel_id=1, source_target_pairs={{0,16},{8,24},{16,0},{24,8},{1,17},{9,25},{17,1},{25,9},{2,18},{10... | collective-permute-start | bytes 2359304 | tf_op jit(solution)/shard_map/F1_dp2/ppermute | solution.py:32
  157.7 12.3 %copy-start.4 = (bf16[768,512]{1,0:T(8,128)(2,1)S(1)}, bf16[768,512]{1,0:T(8,128)(2,1)}, u32[]{:S(2)}) copy-start(bf16[768,512]{1,0:T(8,128)(2,1)} %copy-done.3) | copy-start | bytes 2359300
  174.6 20.0 %collective-permute-start.27 = (bf16[8,3,32,1536]{3,2,1,0:T(8,128)(2,1)}, bf16[8,3,32,1536]{3,2,1,0:T(8,128)(2,1)}, u32[]{:S(2)}, u32[]{:S(2)}) collective-permute-start(bf16[8,3,32,1536]{3,2,1,0:T(8,128)(2,1)} %shard_map.272), channel_id=1, source_target_pairs={{0,8},{8,0},{16,24},{24,16},{1,9},{9,1},{17,25},{25,17},{2,10},{10... | collective-permute-start | bytes 7077896 | tf_op jit(solution)/shard_map/RA_dp1/ppermute | solution.py:32
  180.2 23.6 %collective-permute-start.32 = (bf16[2,4,32,1536]{3,2,1,0:T(8,128)(2,1)}, bf16[2,4,32,1536]{3,2,1,0:T(8,128)(2,1)}, u32[]{:S(2)}, u32[]{:S(2)}) collective-permute-start(bf16[2,4,32,1536]{3,2,1,0:T(8,128)(2,1)} %pad_maximum_fusion.4), channel_id=1, source_target_pairs={{0,1},{1,0},{2,3},{3,2},{4,5},{5,4},{6,7},{7,6},{8,9},{9,8},{10,11... | collective-permute-start | bytes 2359304 | tf_op jit(solution)/shard_map/F1_shard1/ppermute | solution.py:32
  182.7 19.5 %collective-permute-start.29 = (bf16[2,128,384]{2,1,0:T(8,128)(2,1)}, bf16[2,128,384]{2,1,0:T(8,128)(2,1)}, u32[]{:S(2)}, u32[]{:S(2)}) collective-permute-start(bf16[2,128,384]{2,1,0:T(8,128)(2,1)} %pad_maximum_fusion.12), channel_id=1, source_target_pairs={{0,2},{1,3},{2,0},{3,1},{4,6},{5,7},{6,4},{7,5},{8,10},{9,11},{10,... | collective-permute-start | bytes 589832 | tf_op jit(solution)/shard_map/F2_shard2/ppermute | solution.py:32
  183.4 20.4 %collective-permute-start.30 = (bf16[2,128,384]{2,1,0:T(8,128)(2,1)}, bf16[2,128,384]{2,1,0:T(8,128)(2,1)}, u32[]{:S(2)}, u32[]{:S(2)}) collective-permute-start(bf16[2,128,384]{2,1,0:T(8,128)(2,1)} %pad_maximum_fusion.13), channel_id=1, source_target_pairs={{0,4},{1,5},{2,6},{3,7},{4,0},{5,1},{6,2},{7,3},{8,12},{9,13},{10,... | collective-permute-start | bytes 589832 | tf_op jit(solution)/shard_map/F2_shard4/ppermute | solution.py:32
  186.7 17.1 %collective-permute-start.31 = (bf16[2,128,384]{2,1,0:T(8,128)(2,1)}, bf16[2,128,384]{2,1,0:T(8,128)(2,1)}, u32[]{:S(2)}, u32[]{:S(2)}) collective-permute-start(bf16[2,128,384]{2,1,0:T(8,128)(2,1)} %pad_maximum_fusion.14), channel_id=1, source_target_pairs={{0,6},{1,7},{2,4},{3,5},{4,2},{5,3},{6,0},{7,1},{8,14},{9,15},{10,... | collective-permute-start | bytes 589832 | tf_op jit(solution)/shard_map/F2_shard6/ppermute | solution.py:32
  195.7 8.1 %collective-permute-start.33 = (f32[18,768]{1,0:T(8,128)S(1)}, f32[18,768]{1,0:T(8,128)S(1)}, u32[]{:S(2)}, u32[]{:S(2)}) collective-permute-start(f32[18,768]{1,0:T(8,128)S(1)} %concatenate.23), channel_id=1, source_target_pairs={{0,8},{8,0},{16,24},{24,16},{1,9},{9,1},{17,25},{25,17},{2,10},{10... | collective-permute-start | bytes 165896 | tf_op jit(solution)/shard_map/sums_dp1/ppermute | solution.py:32
  202.2 25.8 %collective-permute-start.28 = (bf16[8,32,1536]{2,1,0:T(8,128)(2,1)S(1)}, bf16[8,32,1536]{2,1,0:T(8,128)(2,1)S(1)}, u32[]{:S(2)}, u32[]{:S(2)}) collective-permute-start(bf16[8,32,1536]{2,1,0:T(8,128)(2,1)S(1)} %get-tuple-element.169), channel_id=1, source_target_pairs={{0,16},{8,24},{16,0},{24,8},{1,17},{9,25},{17,1},{25,9},{2,18},{10... | collective-permute-start | bytes 2359304 | tf_op jit(solution)/shard_map/RA_dp2/ppermute | solution.py:32
  206.2 18.0 %collective-permute-start.35 = (f32[18,768]{1,0:T(8,128)S(1)}, f32[18,768]{1,0:T(8,128)S(1)}, u32[]{:S(2)}, u32[]{:S(2)}) collective-permute-start(f32[18,768]{1,0:T(8,128)S(1)} %add.429), channel_id=1, source_target_pairs={{0,16},{8,24},{16,0},{24,8},{1,17},{9,25},{17,1},{25,9},{2,18},{10... | collective-permute-start | bytes 165896 | tf_op jit(solution)/shard_map/sums_dp2/ppermute | solution.py:32
  206.8 24.4 %collective-permute-start.36 = (bf16[2,32,1536]{2,1,0:T(8,128)(2,1)S(1)}, bf16[2,32,1536]{2,1,0:T(8,128)(2,1)S(1)}, u32[]{:S(2)}, u32[]{:S(2)}) collective-permute-start(bf16[2,32,1536]{2,1,0:T(8,128)(2,1)S(1)} %pad_maximum_fusion.15), channel_id=1, source_target_pairs={{0,2},{1,3},{2,0},{3,1},{4,6},{5,7},{6,4},{7,5},{8,10},{9,11},{10,... | collective-permute-start | bytes 589832 | tf_op jit(solution)/shard_map/F1_shard2/ppermute | solution.py:32
  209.9 18.1 %collective-permute-start.34 = (bf16[2,128,384]{2,1,0:T(8,128)(2,1)S(1)}, bf16[2,128,384]{2,1,0:T(8,128)(2,1)S(1)}, u32[]{:S(2)}, u32[]{:S(2)}) collective-permute-start(bf16[2,128,384]{2,1,0:T(8,128)(2,1)S(1)} %add_convert_fusion.2), channel_id=1, source_target_pairs={{0,16},{8,24},{16,0},{24,8},{1,17},{9,25},{17,1},{25,9},{2,18},{10... | collective-permute-start | bytes 589832 | tf_op jit(solution)/shard_map/F2_dp2/ppermute | solution.py:32
  210.5 22.2 %collective-permute-start.37 = (bf16[2,32,1536]{2,1,0:T(8,128)(2,1)S(1)}, bf16[2,32,1536]{2,1,0:T(8,128)(2,1)S(1)}, u32[]{:S(2)}, u32[]{:S(2)}) collective-permute-start(bf16[2,32,1536]{2,1,0:T(8,128)(2,1)S(1)} %pad_maximum_fusion.16), channel_id=1, source_target_pairs={{0,4},{1,5},{2,6},{3,7},{4,0},{5,1},{6,2},{7,3},{8,12},{9,13},{10,... | collective-permute-start | bytes 589832 | tf_op jit(solution)/shard_map/F1_shard4/ppermute | solution.py:32
  228.2 20.8 %collective-permute-start.39 = (bf16[2,4,32,1536]{3,2,1,0:T(8,128)(2,1)S(1)}, bf16[2,4,32,1536]{3,2,1,0:T(8,128)(2,1)S(1)}, u32[]{:S(2)}, u32[]{:S(2)}) collective-permute-start(bf16[2,4,32,1536]{3,2,1,0:T(8,128)(2,1)S(1)} %pad_maximum_fusion.5), channel_id=1, source_target_pairs={{0,1},{1,0},{2,3},{3,2},{4,5},{5,4},{6,7},{7,6},{8,9},{9,8},{10,11... | collective-permute-start | bytes 2359304 | tf_op jit(solution)/shard_map/RA_shard1/ppermute | solution.py:32
  228.9 20.1 %collective-permute-start.40 = (bf16[3,128,384]{2,1,0:T(8,128)(2,1)S(1)}, bf16[3,128,384]{2,1,0:T(8,128)(2,1)S(1)}, u32[]{:S(2)}, u32[]{:S(2)}) collective-permute-start(bf16[3,128,384]{2,1,0:T(8,128)(2,1)S(1)} %pad_maximum_fusion.8), channel_id=1, source_target_pairs={{0,8},{8,0},{16,24},{24,16},{1,9},{9,1},{17,25},{25,17},{2,10},{10... | collective-permute-start | bytes 884744 | tf_op jit(solution)/shard_map/F2_dp1/ppermute | solution.py:32
  229.0 9.3 %collective-permute-start.38 = (bf16[2,32,1536]{2,1,0:T(8,128)(2,1)S(1)}, bf16[2,32,1536]{2,1,0:T(8,128)(2,1)S(1)}, u32[]{:S(2)}, u32[]{:S(2)}) collective-permute-start(bf16[2,32,1536]{2,1,0:T(8,128)(2,1)S(1)} %pad_maximum_fusion.17), channel_id=1, source_target_pairs={{0,6},{1,7},{2,4},{3,5},{4,2},{5,3},{6,0},{7,1},{8,14},{9,15},{10,... | collective-permute-start | bytes 589832 | tf_op jit(solution)/shard_map/F1_shard6/ppermute | solution.py:32
  231.1 17.8 %collective-permute-start.41 = (f32[18,768]{1,0:T(8,128)S(1)}, f32[18,768]{1,0:T(8,128)S(1)}, u32[]{:S(2)}, u32[]{:S(2)}) collective-permute-start(f32[18,768]{1,0:T(8,128)S(1)} %add.442), channel_id=1, source_target_pairs={{0,1},{1,0},{2,3},{3,2},{4,5},{5,4},{6,7},{7,6},{8,9},{9,8},{10,11... | collective-permute-start | bytes 165896 | tf_op jit(solution)/shard_map/sums_shard1/ppermute | solution.py:32
  249.3 13.6 %collective-permute-start.42 = (bf16[2,32,1536]{2,1,0:T(8,128)(2,1)S(1)}, bf16[2,32,1536]{2,1,0:T(8,128)(2,1)S(1)}, u32[]{:S(2)}, u32[]{:S(2)}) collective-permute-start(bf16[2,32,1536]{2,1,0:T(8,128)(2,1)S(1)} %pad_maximum_fusion.18), channel_id=1, source_target_pairs={{0,2},{1,3},{2,0},{3,1},{4,6},{5,7},{6,4},{7,5},{8,10},{9,11},{10,... | collective-permute-start | bytes 589832 | tf_op jit(solution)/shard_map/RA_shard2/ppermute | solution.py:32
  249.4 16.9 %collective-permute-start.43 = (bf16[2,32,1536]{2,1,0:T(8,128)(2,1)S(1)}, bf16[2,32,1536]{2,1,0:T(8,128)(2,1)S(1)}, u32[]{:S(2)}, u32[]{:S(2)}) collective-permute-start(bf16[2,32,1536]{2,1,0:T(8,128)(2,1)S(1)} %pad_maximum_fusion.19), channel_id=1, source_target_pairs={{0,4},{1,5},{2,6},{3,7},{4,0},{5,1},{6,2},{7,3},{8,12},{9,13},{10,... | collective-permute-start | bytes 589832 | tf_op jit(solution)/shard_map/RA_shard4/ppermute | solution.py:32
  252.1 14.3 %collective-permute-start.44 = (bf16[2,32,1536]{2,1,0:T(8,128)(2,1)S(1)}, bf16[2,32,1536]{2,1,0:T(8,128)(2,1)S(1)}, u32[]{:S(2)}, u32[]{:S(2)}) collective-permute-start(bf16[2,32,1536]{2,1,0:T(8,128)(2,1)S(1)} %pad_maximum_fusion.20), channel_id=1, source_target_pairs={{0,6},{1,7},{2,4},{3,5},{4,2},{5,3},{6,0},{7,1},{8,14},{9,15},{10,... | collective-permute-start | bytes 589832 | tf_op jit(solution)/shard_map/RA_shard6/ppermute | solution.py:32
  254.0 12.3 %collective-permute-start.45 = (bf16[2,32,1536]{2,1,0:T(8,128)(2,1)S(1)}, bf16[2,32,1536]{2,1,0:T(8,128)(2,1)S(1)}, u32[]{:S(2)}, u32[]{:S(2)}) collective-permute-start(bf16[2,32,1536]{2,1,0:T(8,128)(2,1)S(1)} %add_convert_fusion.1), channel_id=1, source_target_pairs={{0,16},{8,24},{16,0},{24,8},{1,17},{9,25},{17,1},{25,9},{2,18},{10... | collective-permute-start | bytes 589832 | tf_op jit(solution)/shard_map/F1_dp2/ppermute | solution.py:32
  255.6 7.2 %collective-permute-start.46 = (f32[18,768]{1,0:T(8,128)S(1)}, f32[18,768]{1,0:T(8,128)S(1)}, u32[]{:S(2)}, u32[]{:S(2)}) collective-permute-start(f32[18,768]{1,0:T(8,128)S(1)} %add.460), channel_id=1, source_target_pairs={{0,2},{1,3},{2,0},{3,1},{4,6},{5,7},{6,4},{7,5},{8,10},{9,11},{10,... | collective-permute-start | bytes 165896 | tf_op jit(solution)/shard_map/sums_shard2/ppermute | solution.py:32
  266.5 8.3 %collective-permute-start.47 = (bf16[2,32,1536]{2,1,0:T(8,128)(2,1)S(1)}, bf16[2,32,1536]{2,1,0:T(8,128)(2,1)S(1)}, u32[]{:S(2)}, u32[]{:S(2)}) collective-permute-start(bf16[2,32,1536]{2,1,0:T(8,128)(2,1)S(1)} %add_convert_fusion), channel_id=1, source_target_pairs={{0,16},{8,24},{16,0},{24,8},{1,17},{9,25},{17,1},{25,9},{2,18},{10... | collective-permute-start | bytes 589832 | tf_op jit(solution)/shard_map/RA_dp2/ppermute | solution.py:32
  268.1 6.7 %collective-permute-start.48 = (bf16[3,32,1536]{2,1,0:T(8,128)(2,1)S(1)}, bf16[3,32,1536]{2,1,0:T(8,128)(2,1)S(1)}, u32[]{:S(2)}, u32[]{:S(2)}) collective-permute-start(bf16[3,32,1536]{2,1,0:T(8,128)(2,1)S(1)} %pad_maximum_fusion.9), channel_id=1, source_target_pairs={{0,8},{8,0},{16,24},{24,16},{1,9},{9,1},{17,25},{25,17},{2,10},{10... | collective-permute-start | bytes 884744 | tf_op jit(solution)/shard_map/F1_dp1/ppermute | solution.py:32
  268.3 6.5 %collective-permute-start.49 = (f32[18,768]{1,0:T(8,128)S(1)}, f32[18,768]{1,0:T(8,128)S(1)}, u32[]{:S(2)}, u32[]{:S(2)}) collective-permute-start(f32[18,768]{1,0:T(8,128)S(1)} %add.465), channel_id=1, source_target_pairs={{0,4},{1,5},{2,6},{3,7},{4,0},{5,1},{6,2},{7,3},{8,12},{9,13},{10,... | collective-permute-start | bytes 165896 | tf_op jit(solution)/shard_map/sums_shard4/ppermute | solution.py:32
  272.8 29.9 %copy-start.19 = (f32[384,768]{1,0:T(8,128)}, f32[384,768]{1,0:T(8,128)S(1)}, u32[]{:S(2)}) copy-start(f32[384,768]{1,0:T(8,128)S(1)} %get-tuple-element.204) | copy-start | bytes 3538948
  276.2 2.4 collective-permute-start.50
  277.8 26.8 %copy-start.20 = (f32[96,3072]{1,0:T(8,128)}, f32[96,3072]{1,0:T(8,128)S(1)}, u32[]{:S(2)}) copy-start(f32[96,3072]{1,0:T(8,128)S(1)} %get-tuple-element.206) | copy-start | bytes 3538948
  279.4 20.1 %copy-start.30 = (f32[96,768]{1,0:T(8,128)}, f32[96,768]{1,0:T(8,128)S(1)}, u32[]{:S(2)}) copy-start(f32[96,768]{1,0:T(8,128)S(1)} %get-tuple-element.208) | copy-start | bytes 884740
  280.2 22.4 %copy-start.24 = (f32[96,2304]{1,0:T(8,128)}, f32[96,2304]{1,0:T(8,128)S(1)}, u32[]{:S(2)}) copy-start(f32[96,2304]{1,0:T(8,128)S(1)} %get-tuple-element.210) | copy-start | bytes 2654212
  282.8 3.6 %collective-permute-start.51 = (f32[]{:T(128)}, f32[]{:T(128)}, u32[]{:S(2)}, u32[]{:S(2)}) collective-permute-start(f32[]{:T(128)} %add.472), channel_id=1, source_target_pairs={{0,1},{1,0},{2,3},{3,2},{4,5},{5,4},{6,7},{7,6},{8,9},{9,8},{10,11... | collective-permute-start | bytes 20 | tf_op jit(solution)/shard_map/sums_shard1/ppermute | solution.py:32
  287.1 3.7 %collective-permute-start.52 = (f32[]{:T(128)}, f32[]{:T(128)}, u32[]{:S(2)}, u32[]{:S(2)}) collective-permute-start(f32[]{:T(128)} %add.473), channel_id=1, source_target_pairs={{0,2},{1,3},{2,0},{3,1},{4,6},{5,7},{6,4},{7,5},{8,10},{9,11},{10,... | collective-permute-start | bytes 20 | tf_op jit(solution)/shard_map/sums_shard2/ppermute | solution.py:32
  291.4 4.5 %collective-permute-start.53 = (f32[]{:T(128)}, f32[]{:T(128)}, u32[]{:S(2)}, u32[]{:S(2)}) collective-permute-start(f32[]{:T(128)} %add.474), channel_id=1, source_target_pairs={{0,4},{1,5},{2,6},{3,7},{4,0},{5,1},{6,2},{7,3},{8,12},{9,13},{10,... | collective-permute-start | bytes 20 | tf_op jit(solution)/shard_map/sums_shard4/ppermute | solution.py:32
  (36 other events, 120.8 us)
